TPU v7x, 128 devices: a whole 4x4x4 slice. The times are simulated.
128 devices in a mesh: snap: 4 (over z), tile: 16 (over x, y), level: 2 (over core).
Axes of the slice: x: 4, y: 4, z: 4, core: 2. Of those that a mesh axis runs over, the one named last changes fastest.
Arguments:
- coarse: bfloat16 [4, 262144, 512], P(None, ('tile', 'level'), 'snap'), may hold values from -100 to 100
- fine_cells: bfloat16 [768, 4, 512, 512], P(('tile', 'level'), None, None, 'snap'), may hold values from -6 to 6
- patch_block: int32 [768], replicated, may hold values from 0 to 4095, as said below
- fine_map: int32 [512], replicated, may hold values from 0 to 63, as said below
- field_weight: float32 [4], replicated, may hold values from 0.25 to 4
Outputs:
- gram_matrix: float32 [512, 512], P(('snap', 'tile', 'level'))
- restricted: bfloat16 [4, 2048, 64, 512], P(None, ('tile', 'level'), None, 'snap')
Inputs may be any that keep to these rules, and one draw needn't show every extreme that they name: `patch_block`: all entries are distinct. At most 2 patches of one owner lie in the boxes of one tile owner, and some owner and tile owner reach 2. `fine_map`: each value appears exactly 8 times.
All inputs are finite; a program needn't handle non-finite values.
Results may differ from a plain program's by a relative error of at most 0.001.
Values may be sent and summed in bfloat16 or wider, within the bound.
No kernel may reach another device: no remote copies, remote signals or barrier semaphores. Data moves between devices by JAX's collectives and lax.ppermute only.
A program may use at most 192 MiB of HBM per device.

v0:
```python
import jax
import jax.numpy as jnp
from jax import lax
from jax.sharding import PartitionSpec as P

F = 4
PB = 64
SLOTS = 64


def patch_ranks(patch_block, owners, blocks_dev, per_owner):
    patch_count = patch_block.shape[0]
    target = patch_block // blocks_dev
    owner_grid = target.reshape(owners, per_owner)
    position = jnp.arange(per_owner, dtype=jnp.int32)
    earlier = position[None, :] < position[:, None]
    same_target = owner_grid[:, :, None] == owner_grid[:, None, :]
    rank_same = jnp.sum((same_target & earlier[None]).astype(jnp.int32), axis=2).reshape(
        patch_count
    )
    source = jnp.arange(patch_count, dtype=jnp.int32) // per_owner
    return (target, source, rank_same)


def averaging_table(fine_map):
    table = (fine_map[:, None] == jnp.arange(PB, dtype=jnp.int32)[None, :]).astype(
        jnp.float32
    ) * 0.125
    return table.astype(jnp.bfloat16)


def on_device(coarse, fine_cells, patch_block, fine_map, field_weight):
    owners = lax.axis_size(("tile", "level"))
    own_index = lax.axis_index(("tile", "level"))
    capacity = SLOTS // owners
    per_owner = fine_cells.shape[0]
    blocks_dev = coarse.shape[1] // PB
    snap_local = coarse.shape[2]
    target, source, rank_same = patch_ranks(patch_block, owners, blocks_dev, per_owner)
    send_slot = target * capacity + rank_same
    own_slots = lax.dynamic_slice_in_dim(send_slot, own_index * per_owner, per_owner)
    placement = (jnp.arange(SLOTS, dtype=jnp.int32)[:, None] == own_slots[None, :]).astype(
        jnp.bfloat16
    )
    averaging = averaging_table(fine_map)
    reduced = jnp.einsum(
        "pfes,eb->pfbs", fine_cells, averaging, preferred_element_type=jnp.float32
    ).astype(jnp.bfloat16)
    outgoing = jnp.einsum(
        "qp,pfbs->fqbs", placement, reduced, preferred_element_type=jnp.float32
    ).astype(jnp.bfloat16)
    received = lax.all_to_all(outgoing, ("tile", "level"), split_axis=1, concat_axis=1, tiled=True)
    local_block = patch_block - own_index * blocks_dev
    matches = jnp.arange(blocks_dev, dtype=jnp.int32)[:, None] == local_block[None, :]
    arrival_slot = source * capacity + rank_same + 1
    block_slot = jnp.sum(jnp.where(matches, arrival_slot[None, :], 0), axis=1) - 1
    covered = block_slot >= 0
    padded = jnp.concatenate([received, jnp.zeros_like(received[:, :1])], axis=1)
    picked = jnp.take(padded, jnp.where(covered, block_slot, SLOTS), axis=1)
    coarse_view = coarse.reshape(F, blocks_dev, PB, snap_local)
    composite = jnp.where(covered[None, :, None, None], picked, coarse_view).reshape(coarse.shape)
    cell_rows = lax.all_to_all(composite, "snap", split_axis=1, concat_axis=2, tiled=True)
    per_field = jnp.einsum("fcs,fct->fst", cell_rows, cell_rows, preferred_element_type=jnp.float32)
    cells_all = coarse.shape[1] * owners
    partial_sum = jnp.sum(field_weight[:, None, None] * per_field, axis=0) / (F * cells_all)
    gram_matrix = lax.psum_scatter(
        partial_sum, ("snap", "tile", "level"), scatter_dimension=0, tiled=True
    )
    return (gram_matrix, received)


def solution(mesh):
    return jax.shard_map(
        on_device,
        mesh=mesh,
        in_specs=(
            P(None, ("tile", "level"), "snap"),
            P(("tile", "level"), None, None, "snap"),
            P(),
            P(),
            P(),
        ),
        out_specs=(P(("snap", "tile", "level"), None), P(None, ("tile", "level"), None, "snap")),
        check_vma=False,
    )
```

profile of v0, /device:TPU:1, one launch (start us, length us, event | category | flops | bytes accessed | tf_op | source)
XLA Modules:
  0.0 459.9 jit_solution(13711917863774989505)
XLA Ops:
  7.2 0.7 add_select_fusion
  8.0 0.2 convert_reduce_fusion
  8.4 0.7 broadcast_subtract_fusion
  9.2 6.9 %fusion.2 = bf16[24,4,64,128]{3,2,1,0:T(8,128)(2,1)S(1)} fusion(bf16[24,4,512,128]{3,2,1,0:T(8,128)(2,1)} %param.6, s32[512]{0:T(512)} %param.8), kind=kOutput, calls=%fused_computation.8 | convolution fusion | flops 806191104 | bytes 14157824 | tf_op jit(solution)/shard_map/pfes,eb->pfbs/dot_general | solution.py:46
  16.1 1.6 convert_bitcast_fusion
  17.6 4.7 %copy.27 = bf16[4,64,64,128]{3,2,0,1:T(8,128)(2,1)} copy(bf16[4,64,64,128]{3,1,2,0:T(8,128)(2,1)S(1)} %convert_bitcast_fusion) | data formatting | bytes 8388608 | tf_op jit(solution)/shard_map/convert_element_type | solution.py:51
  22.3 8.6 %all-to-all-start = ((bf16[4,64,64,128]{3,2,0,1:T(8,128)(2,1)}), bf16[4,64,64,128]{3,2,0,1:T(8,128)(2,1)}, u32[]{:S(2)}, u32[]{:S(2)}) async-start(bf16[4,64,64,128]{3,2,0,1:T(8,128)(2,1)} %copy.27), calls=%async_computation | async-start | bytes 8388608 | tf_op jit(solution)/shard_map/all_to_all | solution.py:52
  31.0 0.2 all-reduce.4.cloned.1.call-start
  31.2 0.1 select_reduce_fusion
  31.8 51.4 %all-to-all-done = bf16[4,64,64,128]{3,2,0,1:T(8,128)(2,1)} async-done(((bf16[4,64,64,128]{3,2,0,1:T(8,128)(2,1)}), bf16[4,64,64,128]{3,2,0,1:T(8,128)(2,1)}, u32[]{:S(2)}, u32[]{:S(2)}) %all-to-all-start) | async-done | bytes 4194336 | tf_op jit(solution)/shard_map/all_to_all | solution.py:52
  83.2 3.1 copy.28
  86.4 2.0 copy-done
  88.4 2.9 concatenate.3
  91.3 8.5 %gather_fusion = bf16[128,4,64,128]{3,2,1,0:T(8,128)(2,1)} fusion(bf16[4,65,64,128]{3,2,1,0:T(8,128)(2,1)} %concatenate.3, s32[1024]{0:T(1024)S(1)} %pad_clamp_fusion), kind=kCustom, calls=%fused_computation | custom fusion | bytes 16777728 | tf_op jit(solution)/shard_map/jit(_take)/gather | solution.py:59
  99.8 9.4 %copy.29 = bf16[4,128,64,128]{3,2,1,0:T(8,128)(2,1)} copy(bf16[4,128,64,128]{3,2,0,1:T(8,128)(2,1)} %bitcast.30) | data formatting | bytes 16777216 | tf_op jit(solution)/shard_map/jit(_take)/gather | solution.py:59
  109.2 8.1 %fusion = bf16[4,8192,128]{2,1,0:T(8,128)(2,1)S(1)} fusion(bf16[4,8192,128]{2,1,0:T(8,128)(2,1)} %param.5, bf16[4,128,64,128]{3,2,1,0:T(8,128)(2,1)} %copy.29, pred[8192]{0:T(1024)(128)(4,1)S(1)} %broadcast_in_dim.64, pred[8192]{0:T(1024)(128)(4,1)S(1)} %broadcast_in_dim.60), kind=kLoop, calls=%fused_computation.2 | loop fusion | flops 8388608 | bytes 25182208 | tf_op jit(solution)/shard_map/jit(_where)/select_n | solution.py:61
  117.3 39.9 %copy.30 = bf16[4,8192,128]{2,0,1:T(4,128)(2,1)S(1)} copy(bf16[4,8192,128]{2,1,0:T(8,128)(2,1)S(1)} %fusion) | data formatting | bytes 16777216 | tf_op jit(solution)/shard_map/jit(_where)/select_n | solution.py:61
  157.2 97.4 %all_to_all.23 = bf16[4,8192,128]{2,0,1:T(4,128)(2,1)S(1)} all-to-all(bf16[4,8192,128]{2,0,1:T(4,128)(2,1)S(1)} %copy.30), channel_id=1, replica_groups=mesh['snap'=4,'tile'=16,'level'=2] {'snap'}, dimensions={1} | all-to-all | bytes 16777216 | tf_op jit(solution)/shard_map/all_to_all | solution.py:62
  254.6 24.8 %copy.40 = bf16[4,4,2048,128]{3,1,2,0:T(4,128)(2,1)} copy(bf16[4,4,2048,128]{3,0,2,1:T(4,128)(2,1)S(1)} %bitcast.31) | data formatting | bytes 16777216 | tf_op jit(solution)/shard_map/all_to_all | solution.py:62
  279.5 13.1 %all_to_all.20 = bf16[4,2048,512]{2,1,0:T(8,128)(2,1)} reshape(bf16[4,2048,4,128]{3,2,1,0:T(4,128)(2,1)} %bitcast.32) | data formatting | bytes 16777216 | tf_op jit(solution)/shard_map/all_to_all | solution.py:62
  292.6 10.4 %multiply_reduce_fusion = f32[512,512]{1,0:T(8,128)S(1)} fusion(bf16[4,2048,512]{2,1,0:T(8,128)(2,1)} %all_to_all.20, f32[4]{0:T(128)S(1)} %copy-done.1), kind=kOutput, calls=%fused_computation.4 | convolution fusion | flops 4296802304 | bytes 9437200 | tf_op jit(solution)/shard_map/fcs,fct->fst/dot_general | solution.py:63
  303.0 1.1 broadcast_multiply_fusion
  304.2 147.6 %all-reduce.4.cloned.1.call-done = f32[512,512]{1,0:T(8,128)} async-done(((f32[512,512]{1,0:T(8,128)}), f32[512,512]{1,0:T(8,128)}) %all-reduce.4.cloned.1.call-update) | async-done | bytes 1048592
  451.8 1.3 constant_dynamic-slice_fusion
  (17 shorter events, 0.8 us)
Async XLA Ops:
  22.3 60.9 %all-to-all-start = ((bf16[4,64,64,128]{3,2,0,1:T(8,128)(2,1)}), bf16[4,64,64,128]{3,2,0,1:T(8,128)(2,1)}, u32[]{:S(2)}, u32[]{:S(2)}) async-start(bf16[4,64,64,128]{3,2,0,1:T(8,128)(2,1)} %copy.27), calls=%async_computation | async-start | bytes 8388608 | tf_op jit(solution)/shard_map/all_to_all | solution.py:52
  31.0 420.8 %all-reduce.4.cloned.1.call-start = ((), (), s32[]{:S(2)}) async-start(), calls=%async_computation.2 | async-start | bytes 2097152
  86.4 2.0 copy-start
  279.5 13.1 %copy-start.1 = (f32[4]{0:T(128)S(1)}, f32[4]{0:T(128)}, u32[]{:S(2)}) copy-start(f32[4]{0:T(128)} %param.9) | copy-start | bytes 52
Sparse Core Ops, SparseCore 0:
  304.3 147.4 all-reduce.3
where the time goes:
time: 461 us; the launch traced here: 460 us
  waiting for transfers between devices  199 us (43%)
  local copies, waits for them, and re-layouts  111 us (24%)
  blocking collectives  97.4 us (21%)
  matrix products  18.9 us (4%)
  between operations  14.2 us (3%)
  other arithmetic  10.9 us (2%)
  starting transfers between devices  8.87 us (2%)
    unnamed x2, waiting for transfers between devices  148 us
    all_to_all x1, blocking collectives, on_device(): lax.all_to_all(composite, 'snap', split_axis=1, concat_axis=2, tiled=True)  97.4 us
    all_to_all x1, waiting for transfers between devices, on_device(): lax.all_to_all(outgoing, ('tile', 'level'), split_axis=1, concat_axis=1,...  51.4 us
    select_n x1, local copies, waits for them, and re-layouts, on_device(): jnp.where(covered[None, :, None, None], picked, coarse_view)  39.9 us
    all_to_all x2, local copies, waits for them, and re-layouts, on_device(): lax.all_to_all(composite, 'snap', split_axis=1, concat_axis=2, tiled=True)  37.9 us
    gather x2, local copies, waits for them, and re-layouts, on_device(): picked = jnp.take(padded, jnp.where(covered, block_slot, SLOTS), axis=1)  17.9 us
    dot_general x1, matrix products, on_device(): jnp.einsum('fcs,fct->fst', cell_rows, cell_rows, preferred_element_type=j...  10.4 us
  transfers between devices with their start and end apart: 2, of which 2 were waited for; matrix products, arithmetic and copies ran while one was open for 0% of the time, Pallas kernels for 0%

commit v1 on v0

v1 whole, which is shorter than its diff:
```python
import jax
import jax.numpy as jnp
from jax import lax
from jax.experimental import pallas as pl
from jax.experimental.pallas import tpu as pltpu
from jax.sharding import PartitionSpec as P

F = 4
PB = 64
SLOTS = 64
NZ = 4
OWNERS = 32
LANES = 128
QUARTER = SLOTS // NZ
GROUPS = ((0, 3), (3, 1))
S = NZ * LANES
SEND_ORDER = (1, 3, 2, 0)
XY = ("tile", "level")
ALL = ("snap", "tile", "level")
BF16, F32, I32 = jnp.bfloat16, jnp.float32, jnp.int32
ANY = pl.BlockSpec(memory_space=pl.ANY)
SMEM = pl.BlockSpec(memory_space=pltpu.SMEM)
VMEM = pl.BlockSpec(memory_space=pltpu.VMEM)
PARAMS = pltpu.CompilerParams(vmem_limit_bytes=58 * 2**20)


def cost(bytes_accessed, flops=0):
    return pl.CostEstimate(flops=flops, bytes_accessed=bytes_accessed, transcendentals=0)


def tables(patch_block, own, z, per_owner, blocks_dev):
    k = jnp.arange(SLOTS, dtype=I32)
    order = QUARTER * ((z + k // QUARTER) % NZ) + k % QUARTER
    boxes = jnp.arange(blocks_dev, dtype=I32)
    local = patch_block - own * blocks_dev
    free = jnp.all(local[None, :] != boxes[:, None], axis=1)
    rank_free = jnp.sum((free[None, :] & (boxes[None, :] < boxes[:, None])).astype(I32), axis=1)
    place = jnp.where(free, rank_free, -1)
    first = jnp.sum(jnp.where(place[None, :] == order[:, None], boxes[None, :], 0), axis=1)

    target = patch_block // blocks_dev
    own_target = lax.dynamic_slice_in_dim(target, own * per_owner, per_owner)
    p = jnp.arange(per_owner, dtype=I32)
    same = (own_target[None, :] == own_target[:, None]) & (p[None, :] < p[:, None])
    slot = own_target * (SLOTS // OWNERS) + jnp.sum(same.astype(I32), axis=1)
    has_patch = jnp.any(slot[None, :] == k[:, None], axis=1).astype(I32)

    arrived = jnp.sum((target.reshape(OWNERS, per_owner) == own).astype(I32), axis=1)
    filled = (arrived[:, None] > jnp.arange(SLOTS // OWNERS, dtype=I32)[None, :]).reshape(SLOTS)
    empty_before = jnp.sum(((~filled)[None, :] & (k[None, :] < order[:, None])).astype(I32), axis=1)
    second = jnp.sum(jnp.where(place[None, :] == SLOTS + empty_before[:, None], boxes[None, :], 0), axis=1)
    filled_at = jnp.any(filled[None, :] & (k[None, :] == order[:, None]), axis=1)
    pick = jnp.where(filled_at, -1, second)
    return first, slot, has_patch, order, pick


def stage_out(stage, outs, into, away):
    for n, out in enumerate(outs):
        pltpu.make_async_copy(out, stage.at[n], into.at[n]).wait()
        pltpu.make_async_copy(stage.at[n], out, away.at[n]).start()
    for n, out in enumerate(outs):
        pltpu.make_async_copy(stage.at[n], out, away.at[n]).wait()


def gather_kernel(parts, first_ref, coarse_ref, *rest):
    outs, (stage, into, away) = rest[:-3], rest[-3:]
    for n, r in enumerate(parts):
        for j in range(QUARTER):
            pltpu.make_async_copy(coarse_ref.at[:, first_ref[r * QUARTER + j]], stage.at[n, j], into.at[n]).start()
    stage_out(stage, outs, into, away)


def gather_free(first, coarse, parts):
    shape = (QUARTER, F, PB, LANES)
    return pl.pallas_call(
        lambda *refs: gather_kernel(parts, *refs),
        out_shape=[jax.ShapeDtypeStruct(shape, BF16) for _ in parts],
        in_specs=[SMEM, ANY],
        out_specs=[ANY for _ in parts],
        scratch_shapes=[pltpu.VMEM((len(parts), *shape), BF16)] + [pltpu.SemaphoreType.DMA((NZ,))] * 2,
        compiler_params=PARAMS,
        cost_estimate=cost(2 * len(parts) * QUARTER * F * PB * LANES * 2),
    )(first, coarse)


def restrict_kernel(steps, group, fields, slot_ref, has_ref, map_ref, fine_ref, after_ref, out_ref, averaging, zeros, results, sem):
    step = pl.program_id(0)

    @pl.when(step == 0)
    def _():
        e_of = map_ref[...]
        b = lax.broadcasted_iota(I32, averaging.shape, 0)
        averaging[...] = jnp.where(e_of == b, 0.125, 0.0).astype(BF16)
        zeros[...] = jnp.zeros_like(zeros)
        for q in range(SLOTS):

            @pl.when(has_ref[q] == 0)
            def _(q=q):
                pltpu.make_async_copy(zeros, out_ref.at[q], sem).start()

    for i in range(group):
        p = step * group + i
        wide = jnp.concatenate([fine_ref[i, f] for f in range(fields)], axis=1)
        mean = jnp.dot(averaging[...], wide, preferred_element_type=F32).astype(BF16)
        for f in range(fields):
            results[p, f] = mean[:, f * LANES : (f + 1) * LANES]
        pltpu.make_async_copy(results.at[p], out_ref.at[slot_ref[p]], sem).start()

    @pl.when(step == steps - 1)
    def _():
        pltpu.make_async_copy(out_ref, out_ref, sem).wait()


def restrict(slot, has_patch, fine_map, fine_cells, at, fields, after):
    per_owner, fine = fine_cells.shape[0], fine_cells.shape[2]
    group = 4
    steps = per_owner // group
    return pl.pallas_call(
        lambda *refs: restrict_kernel(steps, group, fields, *refs),
        grid=(steps,),
        out_shape=jax.ShapeDtypeStruct((SLOTS, fields, PB, LANES), BF16),
        in_specs=[
            SMEM,
            SMEM,
            pl.BlockSpec((1, fine), lambda i: (0, 0)),
            pl.BlockSpec((group, fields, fine, LANES), lambda i: (i, at // fields, 0, 0)),
            ANY,
        ],
        out_specs=ANY,
        scratch_shapes=[
            pltpu.VMEM((PB, fine), BF16),
            pltpu.VMEM((fields, PB, LANES), BF16),
            pltpu.VMEM((per_owner, fields, PB, LANES), BF16),
            pltpu.SemaphoreType.DMA,
        ],
        compiler_params=PARAMS,
        cost_estimate=cost(fields * 2**22, 2 * per_owner * fields * PB * fine * LANES),
    )(slot, has_patch, fine_map.reshape(1, fine), fine_cells, after)


def merge_kernel(at, count, order_ref, pick_ref, received_ref, coarse_ref, *rest):
    outs, (stage, into, away) = rest[:-3], rest[-3:]
    fields = pl.ds(at, count)
    for n, r in enumerate(SEND_ORDER):
        for j in range(QUARTER):
            k = r * QUARTER + j
            box = pick_ref[k]

            @pl.when(box < 0)
            def _(n=n, j=j, k=k):
                pltpu.make_async_copy(received_ref.at[order_ref[k]], stage.at[n, j], into.at[n]).start()

            @pl.when(box >= 0)
            def _(n=n, j=j, box=box):
                pltpu.make_async_copy(coarse_ref.at[fields, box], stage.at[n, j], into.at[n]).start()

    stage_out(stage, [outs[r] for r in SEND_ORDER], into, away)


def merge(order, pick, received, coarse, at):
    count = received.shape[1]
    shape = (QUARTER, count, PB, LANES)
    return pl.pallas_call(
        lambda *refs: merge_kernel(at, count, *refs),
        out_shape=[jax.ShapeDtypeStruct(shape, BF16)] * NZ,
        in_specs=[SMEM, SMEM, ANY, ANY],
        out_specs=[ANY] * NZ,
        scratch_shapes=[pltpu.VMEM((NZ, *shape), BF16)] + [pltpu.SemaphoreType.DMA((NZ,))] * 2,
        compiler_params=PARAMS,
        cost_estimate=cost(count * 2**21),
    )(order, pick, received, coarse)


def output_kernel(low_ref, high_ref, out_ref, stage, into, away):
    ins, outs = [], []
    for ref, (at, count) in zip((low_ref, high_ref), GROUPS):
        for i in range(count):
            f = at + i
            ins.append(pltpu.make_async_copy(ref.at[:, i], stage.at[f], into.at[f]))
            outs.append(pltpu.make_async_copy(stage.at[f], out_ref.at[f], away.at[f]))
    for copy in ins:
        copy.start()
    for copy, out in zip(ins, outs):
        copy.wait()
        out.start()
    for out in outs:
        out.wait()


def slot_output(low, high):
    return pl.pallas_call(
        output_kernel,
        out_shape=jax.ShapeDtypeStruct((F, SLOTS, PB, LANES), BF16),
        in_specs=[ANY, ANY],
        out_specs=ANY,
        scratch_shapes=[pltpu.VMEM((F, SLOTS, PB, LANES), BF16)] + [pltpu.SemaphoreType.DMA((F,))] * 2,
        compiler_params=PARAMS,
        cost_estimate=cost(8 * 2**20),
    )(low, high)


def gram_kernel(offset, weight_ref, x0, x1, x2, x3, before_ref, out_ref):
    f = pl.program_id(0)

    @pl.when(f == 0)
    def _():
        out_ref[...] = before_ref[...]

    cells = QUARTER * PB
    wide = jnp.concatenate([x[...].reshape(cells, LANES) for x in (x0, x1, x2, x3)], axis=1)
    product = lax.dot_general(wide, wide, (((0,), (0,)), ((), ())), preferred_element_type=F32)
    for b in range(NZ):
        out_ref[b] += weight_ref[offset + f] * product[:, b * LANES : (b + 1) * LANES]


def first_gram_kernel(weight_ref, x0, x1, x2, x3, out_ref):
    f = pl.program_id(0)

    @pl.when(f == 0)
    def _():
        out_ref[...] = jnp.zeros_like(out_ref)

    cells = QUARTER * PB
    wide = jnp.concatenate([x[...].reshape(cells, LANES) for x in (x0, x1, x2, x3)], axis=1)
    product = lax.dot_general(wide, wide, (((0,), (0,)), ((), ())), preferred_element_type=F32)
    for b in range(NZ):
        out_ref[b] += weight_ref[f] * product[:, b * LANES : (b + 1) * LANES]


def gram(weight, xs, before=None, offset=0):
    fields = xs[0].shape[1]
    block = pl.BlockSpec((QUARTER, 1, PB, LANES), lambda f: (0, f, 0, 0))
    whole = pl.BlockSpec((NZ, S, LANES), lambda f: (0, 0, 0))
    if before is None:
        kernel, more, extra = first_gram_kernel, (), []
    else:
        kernel, more, extra = (lambda *refs: gram_kernel(offset, *refs)), (before,), [whole]
    return pl.pallas_call(
        kernel,
        grid=(fields,),
        out_shape=jax.ShapeDtypeStruct((NZ, S, LANES), F32),
        in_specs=[SMEM] + [block] * NZ + extra,
        out_specs=whole,
        compiler_params=PARAMS,
        cost_estimate=cost(fields * 2**20 + 2**21, 2 * fields * QUARTER * PB * S * S),
    )(weight, *xs, *more)


def pieces_kernel(scale, z_ref, in_ref, out_ref):
    z = z_ref[0]
    rows = S // 128
    for a in range(NZ):
        ga = (a + z) % NZ
        for b in range(NZ):
            gb = (b + z) % NZ
            for i in range(rows):
                part = in_ref[b, pl.ds(a * LANES + i, LANES // rows, stride=rows), :]
                start = ga * (LANES // rows) * 16 + gb * rows + i
                out_ref[pl.ds(start, LANES // rows, stride=16), :] = part * scale


def pieces(z, total, scale):
    return pl.pallas_call(
        lambda *refs: pieces_kernel(scale, *refs),
        out_shape=jax.ShapeDtypeStruct((S * NZ, LANES), F32),
        in_specs=[SMEM, VMEM],
        out_specs=VMEM,
        compiler_params=PARAMS,
        cost_estimate=cost(2 * 2**20),
    )(z.reshape(1), total)


def shift(x, by):
    return lax.ppermute(x, "snap", [(i, (i + by) % NZ) for i in range(NZ)])


def exchange(sends):
    from_below = shift(sends[1], 1)
    from_above = shift(sends[3], 3)
    from_across = shift(sends[2], 2)
    return (sends[0], from_above, from_across, from_below)


def on_device(coarse, fine_cells, patch_block, fine_map, field_weight):
    own = lax.axis_index(XY).astype(I32)
    z = lax.axis_index("snap").astype(I32)
    per_owner = fine_cells.shape[0]
    blocks_dev = coarse.shape[1] // PB
    coarse_boxes = coarse.reshape(F, blocks_dev, PB, LANES)
    first, slot, has_patch, order, pick = tables(patch_block, own, z, per_owner, blocks_dev)

    up, down = gather_free(first, coarse_boxes, (1, 3))
    across, stay = gather_free(first, coarse_boxes, (2, 0))
    group_a = exchange((stay, up, across, down))

    received = []
    for (at, fields), after in zip(GROUPS, (up, across)):
        outgoing = restrict(slot, has_patch, fine_map, fine_cells, at, fields, after)
        if at:
            outgoing, received[0], group_a = lax.optimization_barrier((outgoing, received[0], group_a))
        received.append(lax.all_to_all(outgoing, XY, split_axis=0, concat_axis=0, tiled=True))
    restricted = slot_output(received[0], received[1])

    total = gram(field_weight, group_a)
    for (at, _), arrived in zip(GROUPS, received):
        group = exchange(merge(order, pick, arrived, coarse_boxes, at))
        total = gram(field_weight, group, total, at)

    cells_all = coarse.shape[1] * OWNERS
    shares = pieces(z, total, 1.0 / (F * cells_all))
    collected = lax.all_to_all(shares, ALL, split_axis=0, concat_axis=0, tiled=True)
    summed = jnp.sum(collected.reshape(128, NZ, NZ, LANES), axis=0)
    gram_matrix = summed.transpose(1, 0, 2).reshape(S // 128, S)
    return (gram_matrix, restricted)


def solution(mesh):
    return jax.shard_map(
        on_device,
        mesh=mesh,
        in_specs=(
            P(None, ("tile", "level"), "snap"),
            P(("tile", "level"), None, None, "snap"),
            P(),
            P(),
            P(),
        ),
        out_specs=(P(("snap", "tile", "level"), None), P(None, ("tile", "level"), None, "snap")),
        check_vma=False,
    )
```

time: 461 us -> 179 us (0.39)
  waiting for transfers between devices: 199 us -> 89.8 us
  local copies, waits for them, and re-layouts: 111 us -> 2.95 us
  blocking collectives: 97.4 us -> 0 us
  Pallas kernels: 0 us -> 45.7 us
  starting transfers between devices: 8.87 us -> 33.3 us
  matrix products: 18.9 us -> 0 us
  between operations: 14.2 us -> 0.87 us
  other arithmetic: 10.9 us -> 5.12 us
    unnamed x2 -> x0, waiting for transfers between devices: 148 us -> none
    all_to_all x1 -> x0, blocking collectives: 97.4 us -> none  [on_device(): lax.all_to_all(composite, 'snap', split_axis=1, concat_axis=2, tiled=True)]
    ppermute x0 -> x9, waiting for transfers between devices: none -> 63.1 us  [shift(): return lax.ppermute(x, 'snap', [(i, (i + by) % NZ) for i in range(NZ)])]
    pallas_call x0 -> x11, Pallas kernels: none -> 45.7 us  [the longest x3 14.8 us: gram(): pl.pallas_call(kernel, grid=(fields,), out_shape=jax.ShapeDtypeStruct((NZ...]
    all_to_all x3 -> x0, local copies, waits for them, and re-layouts: 41.1 us -> none  [the longest x2 37.9 us: on_device(): lax.all_to_all(composite, 'snap', split_axis=1, concat_axis=2, tiled=True)]
    select_n x1 -> x0, local copies, waits for them, and re-layouts: 39.9 us -> none  [on_device(): jnp.where(covered[None, :, None, None], picked, coarse_view)]
    all_to_all x1 -> x3, waiting for transfers between devices: 51.4 us -> 26.7 us  [the longest x1 15.6 us: on_device(): lax.all_to_all(shares, ALL, split_axis=0, concat_axis=0, tiled=True)]
    dot_general x3 -> x0, matrix products: 18.9 us -> none  [the longest x1 10.4 us: on_device(): jnp.einsum('fcs,fct->fst', cell_rows, cell_rows, preferred_element_type=j...]
  transfers between devices with their start and end apart: 2 -> 12, of which waited for: 2 -> 7; matrix products, arithmetic and copies ran while one was open for 0% -> 0% of each run, Pallas kernels for 0% -> 16%
where the time goes in v1:
time: 179 us; the launch traced here: 178 us
  waiting for transfers between devices  89.8 us (50%)
  Pallas kernels  45.7 us (26%)
  starting transfers between devices  33.3 us (19%)
  other arithmetic  5.12 us (3%)
  local copies, waits for them, and re-layouts  2.95 us (2%)
    ppermute x9, waiting for transfers between devices, shift(): return lax.ppermute(x, 'snap', [(i, (i + by) % NZ) for i in range(NZ)])  63.1 us
    all_to_all x2, starting transfers between devices, on_device(): lax.all_to_all(outgoing, XY, split_axis=0, concat_axis=0, tiled=True)  16.6 us
    all_to_all x1, waiting for transfers between devices, on_device(): lax.all_to_all(shares, ALL, split_axis=0, concat_axis=0, tiled=True)  15.6 us
    pallas_call x3, Pallas kernels, gram(): pl.pallas_call(kernel, grid=(fields,), out_shape=jax.ShapeDtypeStruct((NZ...  14.8 us
    pallas_call x2, Pallas kernels, restrict(): pl.pallas_call(lambda *refs: restrict_kernel(steps, group, fields, *refs)...  12 us
    all_to_all x2, waiting for transfers between devices, on_device(): lax.all_to_all(outgoing, XY, split_axis=0, concat_axis=0, tiled=True)  11.2 us
    all_to_all x1, starting transfers between devices, on_device(): lax.all_to_all(shares, ALL, split_axis=0, concat_axis=0, tiled=True)  9.6 us
    ppermute x9, starting transfers between devices, shift(): return lax.ppermute(x, 'snap', [(i, (i + by) % NZ) for i in range(NZ)])  7.08 us
  transfers between devices with their start and end apart: 12, of which 7 were waited for; matrix products, arithmetic and copies ran while one was open for 0% of the time, Pallas kernels for 16%

profile of v1, /device:TPU:1, one launch (start us, length us, event | category | flops | bytes accessed | tf_op | source)
XLA Modules:
  0.0 177.7 jit_solution(10952444947353308306)
XLA Ops:
  4.7 3.3 %shard_map.70 = (bf16[16,4,64,128]{3,2,1,0:T(8,128)(2,1)}, bf16[16,4,64,128]{3,2,1,0:T(8,128)(2,1)}) custom-call(s32[64]{0:T(128)} %get-tuple-element.38.refs_0_, bf16[4,128,64,128]{3,2,1,0:T(8,128)(2,1)} %bitcast.9), custom_call_target="tpu_custom_call" | custom-call | bytes 4194304 | tf_op jit(solution)/shard_map/pallas_call | solution.py:75
  8.0 7.2 %shard_map.71 = bf16[64,3,64,128]{3,2,1,0:T(8,128)(2,1)} custom-call(s32[24]{0:T(128)} %copy-done.5, s32[64]{0:T(128)} %convert_element_type.23.refs_1_, s32[1,512]{1,0:T(1,128)} %bitcast.15, bf16[24,4,512,128]{3,2,1,0:T(8,128)(2,1)} %refs_3_.3, bf16[16,4,64,128]{3,2,1,0:T(8,128)(2,1)} %get-tuple-element.21.refs_4_), custom_call_target="tpu_custom_call" | custom-call | flops 603979776 | bytes 12582912 | tf_op jit(solution)/shard_map/pallas_call | solution.py:118
  15.2 8.6 %all-to-all-start = ((bf16[64,3,64,128]{3,2,1,0:T(8,128)(2,1)}), bf16[64,3,64,128]{3,2,1,0:T(8,128)(2,1)S(1)}, u32[]{:S(2)}, u32[]{:S(2)}) async-start(bf16[64,3,64,128]{3,2,1,0:T(8,128)(2,1)} %shard_map.71), calls=%async_computation | async-start | bytes 6291456 | tf_op jit(solution)/shard_map/all_to_all | solution.py:301
  23.8 3.8 %collective-permute-start = (bf16[16,4,64,128]{3,2,1,0:T(8,128)(2,1)}, bf16[16,4,64,128]{3,2,1,0:T(8,128)(2,1)S(1)}, u32[]{:S(2)}, u32[]{:S(2)}) collective-permute-start(bf16[16,4,64,128]{3,2,1,0:T(8,128)(2,1)} %get-tuple-element.23), channel_id=1, source_target_pairs={{0,96},{32,0},{64,32},{96,64},{1,97},{33,1},{65,33},{97,65},{2,98}... | collective-permute-start | bytes 3145736 | tf_op jit(solution)/shard_map/ppermute | solution.py:274
  27.6 3.3 %shard_map.68 = (bf16[16,4,64,128]{3,2,1,0:T(8,128)(2,1)}, bf16[16,4,64,128]{3,2,1,0:T(8,128)(2,1)}) custom-call(s32[64]{0:T(128)} %get-tuple-element.38.refs_0_, bf16[4,128,64,128]{3,2,1,0:T(8,128)(2,1)} %bitcast.10), custom_call_target="tpu_custom_call" | custom-call | bytes 4194304 | tf_op jit(solution)/shard_map/pallas_call | solution.py:75
  31.8 4.9 %shard_map.69 = bf16[64,1,64,128]{3,2,1,0:T(8,128)(2,1)} custom-call(s32[24]{0:T(128)} %copy-done.5, s32[64]{0:T(128)} %convert_element_type.23.refs_1_, s32[1,512]{1,0:T(1,128)} %bitcast.16, bf16[24,4,512,128]{3,2,1,0:T(8,128)(2,1)} %refs_3_.3, bf16[16,4,64,128]{3,2,1,0:T(8,128)(2,1)} %get-tuple-element.20.refs_4_), custom_call_target="tpu_custom_call" | custom-call | flops 201326592 | bytes 4194304 | tf_op jit(solution)/shard_map/pallas_call | solution.py:118
  36.7 36.0 %collective-permute-done.x1 = bf16[16,4,64,128]{3,2,1,0:T(8,128)(2,1)S(1)} collective-permute-done((bf16[16,4,64,128]{3,2,1,0:T(8,128)(2,1)}, bf16[16,4,64,128]{3,2,1,0:T(8,128)(2,1)S(1)}, u32[]{:S(2)}, u32[]{:S(2)}) %collective-permute-start) | collective-permute-done | bytes 1048608 | tf_op jit(solution)/shard_map/ppermute | solution.py:274
  72.7 1.0 copy-done.7
  73.8 5.8 %collective-permute-done.2.x3 = bf16[16,4,64,128]{3,2,1,0:T(8,128)(2,1)} collective-permute-done((bf16[16,4,64,128]{3,2,1,0:T(8,128)(2,1)S(1)}, bf16[16,4,64,128]{3,2,1,0:T(8,128)(2,1)}, u32[]{:S(2)}, u32[]{:S(2)}) %collective-permute-start.2) | collective-permute-done | bytes 1048608 | tf_op jit(solution)/shard_map/ppermute | solution.py:274
  79.5 8.0 %all-to-all-start.1 = ((bf16[64,1,64,128]{3,2,1,0:T(8,128)(2,1)}), bf16[64,1,64,128]{3,2,1,0:T(8,128)(2,1)}, u32[]{:S(2)}, u32[]{:S(2)}) async-start(bf16[64,1,64,128]{3,2,1,0:T(8,128)(2,1)} %shard_map.69), calls=%async_computation.1 | async-start | bytes 2097152 | tf_op jit(solution)/shard_map/all_to_all | solution.py:301
  88.2 3.5 %shard_map.73 = (bf16[16,3,64,128]{3,2,1,0:T(8,128)(2,1)}, bf16[16,3,64,128]{3,2,1,0:T(8,128)(2,1)}, bf16[16,3,64,128]{3,2,1,0:T(8,128)(2,1)}, bf16[16,3,64,128]{3,2,1,0:T(8,128)(2,1)}) custom-call(s32[64]{0:T(128)} %copy-done.6, s32[64]{0:T(128)} %broadcast_select_fusion.1.refs_1_, bf16[64,3,64,128]{3,2,1,0:T(8,128)(2,1)} %copy-done, ...), custom_call_target="tpu_custom_call" | custom-call | bytes 6291456 | tf_op jit(solution)/shard_map/pallas_call | solution.py:163
  93.3 11.2 %all-to-all-done.1.refs_2_.high_ref = bf16[64,1,64,128]{3,2,1,0:T(8,128)(2,1)} async-done(((bf16[64,1,64,128]{3,2,1,0:T(8,128)(2,1)}), bf16[64,1,64,128]{3,2,1,0:T(8,128)(2,1)}, u32[]{:S(2)}, u32[]{:S(2)}) %all-to-all-start.1) | async-done | bytes 1048608 | tf_op jit(solution)/shard_map/all_to_all | solution.py:301
  104.5 2.7 %shard_map.72 = (bf16[16,1,64,128]{3,2,1,0:T(8,128)(2,1)}, bf16[16,1,64,128]{3,2,1,0:T(8,128)(2,1)}, bf16[16,1,64,128]{3,2,1,0:T(8,128)(2,1)}, bf16[16,1,64,128]{3,2,1,0:T(8,128)(2,1)}) custom-call(s32[64]{0:T(128)} %copy-done.6, s32[64]{0:T(128)} %broadcast_select_fusion.1.refs_1_, bf16[64,1,64,128]{3,2,1,0:T(8,128)(2,1)} %all-to-all-done.1.refs_2_.high_ref, ...), custom_call_target="tpu_custom_call" | custom-call | bytes 2097152 | tf_op jit(solution)/shard_map/pallas_call | solution.py:163
  108.0 2.9 %collective-permute-done.6.refs_2_ = bf16[16,3,64,128]{3,2,1,0:T(8,128)(2,1)S(1)} collective-permute-done((bf16[16,3,64,128]{3,2,1,0:T(8,128)(2,1)}, bf16[16,3,64,128]{3,2,1,0:T(8,128)(2,1)S(1)}, u32[]{:S(2)}, u32[]{:S(2)}) %collective-permute-start.6) | collective-permute-done | bytes 786464 | tf_op jit(solution)/shard_map/ppermute | solution.py:274
  110.9 6.1 %shard_map.74.refs_5_ = f32[4,512,128]{2,1,0:T(8,128)} custom-call(f32[4]{0:T(128)} %refs_0_.3, bf16[16,4,64,128]{3,2,1,0:T(8,128)(2,1)} %get-tuple-element.34.x0, bf16[16,4,64,128]{3,2,1,0:T(8,128)(2,1)} %copy-done.7, bf16[16,4,64,128]{3,2,1,0:T(8,128)(2,1)} %collective-permute-done.1.x2, bf16[16,4,64,128]{3,2,1,0:T(8,128)(2,1)} %collective-permute-done.2.x3), custom_call_target="tpu_custom_call" | custom-call | flops 2147483648 | bytes 6291456 | tf_op jit(solution)/shard_map/pallas_call | solution.py:238
  117.0 14.5 %collective-permute-done.8.refs_4_ = bf16[16,3,64,128]{3,2,1,0:T(8,128)(2,1)S(1)} collective-permute-done((bf16[16,3,64,128]{3,2,1,0:T(8,128)(2,1)}, bf16[16,3,64,128]{3,2,1,0:T(8,128)(2,1)S(1)}, u32[]{:S(2)}, u32[]{:S(2)}) %collective-permute-start.8) | collective-permute-done | bytes 786464 | tf_op jit(solution)/shard_map/ppermute | solution.py:274
  131.5 0.9 copy-done.10
  132.4 5.4 %shard_map.75.refs_5_ = f32[4,512,128]{2,1,0:T(8,128)} custom-call(f32[4]{0:T(128)} %refs_0_.3, bf16[16,3,64,128]{3,2,1,0:T(8,128)(2,1)} %get-tuple-element.30.refs_1_, bf16[16,3,64,128]{3,2,1,0:T(8,128)(2,1)} %copy-done.8, bf16[16,3,64,128]{3,2,1,0:T(8,128)(2,1)} %copy-done.9, bf16[16,3,64,128]{3,2,1,0:T(8,128)(2,1)} %copy-done.10, ...), custom_call_target="tpu_custom_call" | custom-call | flops 1610612736 | bytes 5242880 | tf_op jit(solution)/shard_map/pallas_call | solution.py:238
  137.9 3.9 %collective-permute-done.5.refs_4_ = bf16[16,1,64,128]{3,2,1,0:T(8,128)(2,1)S(1)} collective-permute-done((bf16[16,1,64,128]{3,2,1,0:T(8,128)(2,1)}, bf16[16,1,64,128]{3,2,1,0:T(8,128)(2,1)S(1)}, u32[]{:S(2)}, u32[]{:S(2)}) %collective-permute-start.5) | collective-permute-done | bytes 262176 | tf_op jit(solution)/shard_map/ppermute | solution.py:274
  142.4 3.3 %shard_map.76.refs_1_ = f32[4,512,128]{2,1,0:T(8,128)} custom-call(f32[4]{0:T(128)} %refs_0_.3, bf16[16,1,64,128]{3,2,1,0:T(8,128)(2,1)} %get-tuple-element.25.refs_1_, bf16[16,1,64,128]{3,2,1,0:T(8,128)(2,1)} %copy-done.2, bf16[16,1,64,128]{3,2,1,0:T(8,128)(2,1)} %copy-done.3, bf16[16,1,64,128]{3,2,1,0:T(8,128)(2,1)} %copy-done.4, ...), custom_call_target="tpu_custom_call" | custom-call | flops 536870912 | bytes 3145728 | tf_op jit(solution)/shard_map/pallas_call | solution.py:238
  145.7 2.7 %shard_map.77 = f32[2048,128]{1,0:T(8,128)} custom-call(s32[1]{0:T(128)} %bitcast.refs_0_, f32[4,512,128]{2,1,0:T(8,128)} %shard_map.76.refs_1_), custom_call_target="tpu_custom_call" | custom-call | bytes 2097152 | tf_op jit(solution)/shard_map/pallas_call | solution.py:263
  148.4 9.6 %all-to-all-start.2 = ((f32[128,16,128]{2,1,0:T(8,128)}), f32[128,16,128]{2,1,0:T(8,128)S(1)}, u32[]{:S(2)}, u32[]{:S(2)}) async-start(f32[128,16,128]{2,1,0:T(8,128)} %bitcast.13), calls=%async_computation.2 | async-start | bytes 2097152 | tf_op jit(solution)/shard_map/all_to_all | solution.py:311
  158.0 3.3 %shard_map.78 = bf16[4,64,64,128]{3,2,1,0:T(8,128)(2,1)} custom-call(bf16[64,3,64,128]{3,2,1,0:T(8,128)(2,1)} %copy-done, bf16[64,1,64,128]{3,2,1,0:T(8,128)(2,1)} %all-to-all-done.1.refs_2_.high_ref), custom_call_target="tpu_custom_call" | custom-call | bytes 8388608 | tf_op jit(solution)/shard_map/pallas_call | solution.py:191
  161.4 15.6 %all-to-all-done.2 = f32[128,16,128]{2,1,0:T(8,128)S(1)} async-done(((f32[128,16,128]{2,1,0:T(8,128)}), f32[128,16,128]{2,1,0:T(8,128)S(1)}, u32[]{:S(2)}, u32[]{:S(2)}) %all-to-all-start.2) | async-done | bytes 1048608 | tf_op jit(solution)/shard_map/all_to_all | solution.py:311
  (55 shorter events, 9.4 us)
Async XLA Ops:
  0.7 86.9 %copy-start.6 = (s32[64]{0:T(128)}, s32[64]{0:T(128)S(1)}, u32[]{:S(2)}) copy-start(s32[64]{0:T(128)S(1)} %fusion.9.refs_0_) | copy-start | bytes 772
  3.3 4.7 %copy-start.5 = (s32[24]{0:T(128)}, s32[24]{0:T(128)S(1)}, u32[]{:S(2)}) copy-start(s32[24]{0:T(128)S(1)} %multiply_add_fusion.refs_0_) | copy-start | bytes 292
  15.2 64.4 %all-to-all-start = ((bf16[64,3,64,128]{3,2,1,0:T(8,128)(2,1)}), bf16[64,3,64,128]{3,2,1,0:T(8,128)(2,1)S(1)}, u32[]{:S(2)}, u32[]{:S(2)}) async-start(bf16[64,3,64,128]{3,2,1,0:T(8,128)(2,1)} %shard_map.71), calls=%async_computation | async-start | bytes 6291456 | tf_op jit(solution)/shard_map/all_to_all | solution.py:301
  23.8 7.2 %copy-start.1 = (bf16[16,4,64,128]{3,2,1,0:T(8,128)(2,1)S(1)}, bf16[16,4,64,128]{3,2,1,0:T(8,128)(2,1)}, u32[]{:S(2)}) copy-start(bf16[16,4,64,128]{3,2,1,0:T(8,128)(2,1)} %get-tuple-element.21.refs_4_) | copy-start | bytes 3145732
  23.8 48.9 %collective-permute-start = (bf16[16,4,64,128]{3,2,1,0:T(8,128)(2,1)}, bf16[16,4,64,128]{3,2,1,0:T(8,128)(2,1)S(1)}, u32[]{:S(2)}, u32[]{:S(2)}) collective-permute-start(bf16[16,4,64,128]{3,2,1,0:T(8,128)(2,1)} %get-tuple-element.23), channel_id=1, source_target_pairs={{0,96},{32,0},{64,32},{96,64},{1,97},{33,1},{65,33},{97,65},{2,98}... | collective-permute-start | bytes 3145736 | tf_op jit(solution)/shard_map/ppermute | solution.py:274
  30.9 41.8 %collective-permute-start.1 = (bf16[16,4,64,128]{3,2,1,0:T(8,128)(2,1)}, bf16[16,4,64,128]{3,2,1,0:T(8,128)(2,1)}, u32[]{:S(2)}, u32[]{:S(2)}) collective-permute-start(bf16[16,4,64,128]{3,2,1,0:T(8,128)(2,1)} %get-tuple-element.20.refs_4_), channel_id=1, source_target_pairs={{0,64},{32,96},{64,0},{96,32},{1,65},{33,97},{65,1},{97,33},{2,66}... | collective-permute-start | bytes 3145736 | tf_op jit(solution)/shard_map/ppermute | solution.py:274
  31.0 48.5 %collective-permute-start.2 = (bf16[16,4,64,128]{3,2,1,0:T(8,128)(2,1)S(1)}, bf16[16,4,64,128]{3,2,1,0:T(8,128)(2,1)}, u32[]{:S(2)}, u32[]{:S(2)}) collective-permute-start(bf16[16,4,64,128]{3,2,1,0:T(8,128)(2,1)S(1)} %copy-done.1), channel_id=1, source_target_pairs={{0,32},{32,64},{64,96},{96,0},{1,33},{33,65},{65,97},{97,1},{2,34}... | collective-permute-start | bytes 3145736 | tf_op jit(solution)/shard_map/ppermute | solution.py:274
  72.7 1.1 copy-start.7
  79.5 8.7 %copy-start = (bf16[64,3,64,128]{3,2,1,0:T(8,128)(2,1)}, bf16[64,3,64,128]{3,2,1,0:T(8,128)(2,1)S(1)}, u32[]{:S(2)}) copy-start(bf16[64,3,64,128]{3,2,1,0:T(8,128)(2,1)S(1)} %all-to-all-done.refs_2_.low_ref) | copy-start | bytes 9437188
  79.5 24.9 %all-to-all-start.1 = ((bf16[64,1,64,128]{3,2,1,0:T(8,128)(2,1)}), bf16[64,1,64,128]{3,2,1,0:T(8,128)(2,1)}, u32[]{:S(2)}, u32[]{:S(2)}) async-start(bf16[64,1,64,128]{3,2,1,0:T(8,128)(2,1)} %shard_map.69), calls=%async_computation.1 | async-start | bytes 2097152 | tf_op jit(solution)/shard_map/all_to_all | solution.py:301
  91.8 19.1 %collective-permute-start.6 = (bf16[16,3,64,128]{3,2,1,0:T(8,128)(2,1)}, bf16[16,3,64,128]{3,2,1,0:T(8,128)(2,1)S(1)}, u32[]{:S(2)}, u32[]{:S(2)}) collective-permute-start(bf16[16,3,64,128]{3,2,1,0:T(8,128)(2,1)} %get-tuple-element.31), channel_id=1, source_target_pairs={{0,96},{32,0},{64,32},{96,64},{1,97},{33,1},{65,33},{97,65},{2,98}... | collective-permute-start | bytes 2359304 | tf_op jit(solution)/shard_map/ppermute | solution.py:274
  92.6 24.4 %collective-permute-start.7 = (bf16[16,3,64,128]{3,2,1,0:T(8,128)(2,1)}, bf16[16,3,64,128]{3,2,1,0:T(8,128)(2,1)S(1)}, u32[]{:S(2)}, u32[]{:S(2)}) collective-permute-start(bf16[16,3,64,128]{3,2,1,0:T(8,128)(2,1)} %get-tuple-element.32), channel_id=1, source_target_pairs={{0,64},{32,96},{64,0},{96,32},{1,65},{33,97},{65,1},{97,33},{2,66}... | collective-permute-start | bytes 2359304 | tf_op jit(solution)/shard_map/ppermute | solution.py:274
  92.6 38.9 %collective-permute-start.8 = (bf16[16,3,64,128]{3,2,1,0:T(8,128)(2,1)}, bf16[16,3,64,128]{3,2,1,0:T(8,128)(2,1)S(1)}, u32[]{:S(2)}, u32[]{:S(2)}) collective-permute-start(bf16[16,3,64,128]{3,2,1,0:T(8,128)(2,1)} %get-tuple-element.33), channel_id=1, source_target_pairs={{0,32},{32,64},{64,96},{96,0},{1,33},{33,65},{65,97},{97,1},{2,34}... | collective-permute-start | bytes 2359304 | tf_op jit(solution)/shard_map/ppermute | solution.py:274
  107.2 30.7 %collective-permute-start.3 = (bf16[16,1,64,128]{3,2,1,0:T(8,128)(2,1)}, bf16[16,1,64,128]{3,2,1,0:T(8,128)(2,1)S(1)}, u32[]{:S(2)}, u32[]{:S(2)}) collective-permute-start(bf16[16,1,64,128]{3,2,1,0:T(8,128)(2,1)} %get-tuple-element.26), channel_id=1, source_target_pairs={{0,96},{32,0},{64,32},{96,64},{1,97},{33,1},{65,33},{97,65},{2,98}... | collective-permute-start | bytes 786440 | tf_op jit(solution)/shard_map/ppermute | solution.py:274
  108.0 29.9 %collective-permute-start.4 = (bf16[16,1,64,128]{3,2,1,0:T(8,128)(2,1)}, bf16[16,1,64,128]{3,2,1,0:T(8,128)(2,1)S(1)}, u32[]{:S(2)}, u32[]{:S(2)}) collective-permute-start(bf16[16,1,64,128]{3,2,1,0:T(8,128)(2,1)} %get-tuple-element.27), channel_id=1, source_target_pairs={{0,64},{32,96},{64,0},{96,32},{1,65},{33,97},{65,1},{97,33},{2,66}... | collective-permute-start | bytes 786440 | tf_op jit(solution)/shard_map/ppermute | solution.py:274
  110.9 20.7 %copy-start.8 = (bf16[16,3,64,128]{3,2,1,0:T(8,128)(2,1)}, bf16[16,3,64,128]{3,2,1,0:T(8,128)(2,1)S(1)}, u32[]{:S(2)}) copy-start(bf16[16,3,64,128]{3,2,1,0:T(8,128)(2,1)S(1)} %collective-permute-done.6.refs_2_) | copy-start | bytes 2359300
  110.9 30.9 %collective-permute-start.5 = (bf16[16,1,64,128]{3,2,1,0:T(8,128)(2,1)}, bf16[16,1,64,128]{3,2,1,0:T(8,128)(2,1)S(1)}, u32[]{:S(2)}, u32[]{:S(2)}) collective-permute-start(bf16[16,1,64,128]{3,2,1,0:T(8,128)(2,1)} %get-tuple-element.28), channel_id=1, source_target_pairs={{0,32},{32,64},{64,96},{96,0},{1,33},{33,65},{65,97},{97,1},{2,34}... | collective-permute-start | bytes 786440 | tf_op jit(solution)/shard_map/ppermute | solution.py:274
  117.0 14.5 %copy-start.9 = (bf16[16,3,64,128]{3,2,1,0:T(8,128)(2,1)}, bf16[16,3,64,128]{3,2,1,0:T(8,128)(2,1)S(1)}, u32[]{:S(2)}) copy-start(bf16[16,3,64,128]{3,2,1,0:T(8,128)(2,1)S(1)} %collective-permute-done.7.refs_3_) | copy-start | bytes 2359300
  131.5 0.9 copy-start.10
  137.8 3.9 %copy-start.2 = (bf16[16,1,64,128]{3,2,1,0:T(8,128)(2,1)}, bf16[16,1,64,128]{3,2,1,0:T(8,128)(2,1)S(1)}, u32[]{:S(2)}) copy-start(bf16[16,1,64,128]{3,2,1,0:T(8,128)(2,1)S(1)} %collective-permute-done.3.refs_2_) | copy-start | bytes 786436
  137.9 3.9 %copy-start.3 = (bf16[16,1,64,128]{3,2,1,0:T(8,128)(2,1)}, bf16[16,1,64,128]{3,2,1,0:T(8,128)(2,1)S(1)}, u32[]{:S(2)}) copy-start(bf16[16,1,64,128]{3,2,1,0:T(8,128)(2,1)S(1)} %collective-permute-done.4.refs_3_) | copy-start | bytes 786436
  141.7 0.7 copy-start.4
  148.4 28.5 %all-to-all-start.2 = ((f32[128,16,128]{2,1,0:T(8,128)}), f32[128,16,128]{2,1,0:T(8,128)S(1)}, u32[]{:S(2)}, u32[]{:S(2)}) async-start(f32[128,16,128]{2,1,0:T(8,128)} %bitcast.13), calls=%async_computation.2 | async-start | bytes 2097152 | tf_op jit(solution)/shard_map/all_to_all | solution.py:311

commit v2 on v1

v2 whole, which is shorter than its diff:
```python
import jax
import jax.numpy as jnp
from jax import lax
from jax.experimental import pallas as pl
from jax.experimental.pallas import tpu as pltpu
from jax.sharding import PartitionSpec as P

F = 4
PB = 64
SLOTS = 64
NZ = 4
OWNERS = 32
LANES = 128
QUARTER = SLOTS // NZ
EARLY = 2
S = NZ * LANES
SEND_ORDER = (2, 1, 3, 0)
GRAM_ORDER = (0, 2, 1, 3)
XY = ("tile", "level")
ALL = ("snap", "tile", "level")
BF16, F32, I32 = jnp.bfloat16, jnp.float32, jnp.int32
ANY = pl.BlockSpec(memory_space=pl.ANY)
SMEM = pl.BlockSpec(memory_space=pltpu.SMEM)
VMEM = pl.BlockSpec(memory_space=pltpu.VMEM)
PARAMS = pltpu.CompilerParams(vmem_limit_bytes=58 * 2**20)


def cost(bytes_accessed, flops=0):
    return pl.CostEstimate(flops=flops, bytes_accessed=bytes_accessed, transcendentals=0)


def tables(patch_block, own, z, per_owner, blocks_dev):
    k = jnp.arange(SLOTS, dtype=I32)
    order = QUARTER * ((z + k // QUARTER) % NZ) + k % QUARTER
    boxes = jnp.arange(blocks_dev, dtype=I32)
    local = patch_block - own * blocks_dev
    free = jnp.all(local[None, :] != boxes[:, None], axis=1)
    rank_free = jnp.sum((free[None, :] & (boxes[None, :] < boxes[:, None])).astype(I32), axis=1)
    place = jnp.where(free, rank_free, -1)
    first = jnp.sum(jnp.where(place[None, :] == order[:, None], boxes[None, :], 0), axis=1)

    target = lax.shift_right_logical(patch_block, jnp.int32(blocks_dev.bit_length() - 1))
    own_target = lax.dynamic_slice_in_dim(target, own * per_owner, per_owner)
    p = jnp.arange(per_owner, dtype=I32)
    same = (own_target[None, :] == own_target[:, None]) & (p[None, :] < p[:, None])
    slot = own_target * (SLOTS // OWNERS) + jnp.sum(same.astype(I32), axis=1)
    has_patch = jnp.any(slot[None, :] == k[:, None], axis=1).astype(I32)

    arrived = jnp.sum((target.reshape(OWNERS, per_owner) == own).astype(I32), axis=1)
    filled = (arrived[:, None] > jnp.arange(SLOTS // OWNERS, dtype=I32)[None, :]).reshape(SLOTS)
    empty_before = jnp.sum(((~filled)[None, :] & (k[None, :] < order[:, None])).astype(I32), axis=1)
    second = jnp.sum(jnp.where(place[None, :] == SLOTS + empty_before[:, None], boxes[None, :], 0), axis=1)
    filled_at = jnp.any(filled[None, :] & (k[None, :] == order[:, None]), axis=1)
    pick = jnp.where(filled_at, -1, second)
    late = jnp.sum(jnp.where(place[None, :] == SLOTS + order[:, None], boxes[None, :] + 1, 0), axis=1) - 1
    return first, slot, has_patch, order, pick, late


def stage_out(stage, outs, into, away):
    for n, out in enumerate(outs):
        pltpu.make_async_copy(out, stage.at[n], into.at[n]).wait()
        pltpu.make_async_copy(stage.at[n], out, away.at[n]).start()
    for n, out in enumerate(outs):
        pltpu.make_async_copy(stage.at[n], out, away.at[n]).wait()


def gather_kernel(parts, first_ref, coarse_ref, after_ref, *rest):
    outs, (stage, into, away) = rest[:-3], rest[-3:]
    for n, r in enumerate(parts):
        for j in range(QUARTER):
            pltpu.make_async_copy(coarse_ref.at[:, first_ref[r * QUARTER + j]], stage.at[n, j], into.at[n]).start()
    stage_out(stage, outs, into, away)


def gather_free(first, coarse, parts, after):
    shape = (QUARTER, F, PB, LANES)
    return pl.pallas_call(
        lambda *refs: gather_kernel(parts, *refs),
        out_shape=[jax.ShapeDtypeStruct(shape, BF16) for _ in parts],
        in_specs=[SMEM, ANY, ANY],
        out_specs=[ANY for _ in parts],
        scratch_shapes=[pltpu.VMEM((len(parts), *shape), BF16)] + [pltpu.SemaphoreType.DMA((NZ,))] * 2,
        compiler_params=PARAMS,
        cost_estimate=cost(2 * len(parts) * QUARTER * F * PB * LANES * 2),
    )(first, coarse, after)


def restrict_kernel(steps, group, fields, slot_ref, has_ref, map_ref, fine_ref, after_ref, out_ref, plain_ref, averaging, zeros, results, sem, plain_sem):
    step = pl.program_id(0)

    @pl.when(step == 0)
    def _():
        e_of = map_ref[...]
        b = lax.broadcasted_iota(I32, averaging.shape, 0)
        averaging[...] = jnp.where(e_of == b, 0.125, 0.0).astype(BF16)
        zeros[...] = jnp.zeros_like(zeros)
        for q in range(SLOTS):

            @pl.when(has_ref[q] == 0)
            def _(q=q):
                pltpu.make_async_copy(zeros, out_ref.at[q], sem).start()

    for i in range(group):
        p = step * group + i
        wide = jnp.concatenate([fine_ref[i, f] for f in range(fields)], axis=1)
        mean = jnp.dot(averaging[...], wide, preferred_element_type=F32).astype(BF16)
        for f in range(fields):
            results[p, f] = mean[:, f * LANES : (f + 1) * LANES]
        pltpu.make_async_copy(results.at[p], out_ref.at[slot_ref[p]], sem).start()

    @pl.when(step == steps - 1)
    def _():
        plain = pltpu.make_async_copy(results.at[:, pl.ds(EARLY, fields - EARLY)], plain_ref, plain_sem)
        plain.start()
        plain.wait()
        pltpu.make_async_copy(out_ref, out_ref, sem).wait()


def restrict(slot, has_patch, fine_map, fine_cells, after):
    per_owner, fields, fine, _ = fine_cells.shape
    group = 4
    steps = per_owner // group
    return pl.pallas_call(
        lambda *refs: restrict_kernel(steps, group, fields, *refs),
        grid=(steps,),
        out_shape=[
            jax.ShapeDtypeStruct((SLOTS, fields, PB, LANES), BF16),
            jax.ShapeDtypeStruct((per_owner, fields - EARLY, PB, LANES), BF16),
        ],
        in_specs=[
            SMEM,
            SMEM,
            pl.BlockSpec((1, fine), lambda i: (0, 0)),
            pl.BlockSpec((group, fields, fine, LANES), lambda i: (i, 0, 0, 0)),
            ANY,
        ],
        out_specs=[ANY, ANY],
        scratch_shapes=[
            pltpu.VMEM((PB, fine), BF16),
            pltpu.VMEM((fields, PB, LANES), BF16),
            pltpu.VMEM((per_owner, fields, PB, LANES), BF16),
            pltpu.SemaphoreType.DMA,
            pltpu.SemaphoreType.DMA,
        ],
        compiler_params=PARAMS,
        cost_estimate=cost(fields * 2**22, 2 * per_owner * fields * PB * fine * LANES),
    )(slot, has_patch, fine_map.reshape(1, fine), fine_cells, after)


def local_kernel(z_ref, late_ref, first_ref, patches_ref, coarse_ref, *rest):
    *outs, stay_ref, stage, stay, into, away, stay_sem = rest
    own = patches_ref.shape[0] // NZ
    for n, r in enumerate(SEND_ORDER):
        for j in range(QUARTER):
            box = jnp.maximum(late_ref[r * QUARTER + j], 0)
            pltpu.make_async_copy(coarse_ref.at[pl.ds(EARLY, F - EARLY), box], stage.at[n, j], into.at[n]).start()
        share = pl.ds((z_ref[0] + r) % NZ * own, own)
        pltpu.make_async_copy(patches_ref.at[share], stage.at[n, pl.ds(QUARTER, own)], into.at[n]).start()
    for j in range(QUARTER):
        pltpu.make_async_copy(coarse_ref.at[:, first_ref[j]], stay.at[j], stay_sem.at[0]).start()
    for n, r in enumerate(SEND_ORDER):
        pltpu.make_async_copy(outs[r], stage.at[n], into.at[n]).wait()
        for j in range(QUARTER):

            @pl.when(late_ref[r * QUARTER + j] < 0)
            def _(n=n, j=j):
                stage[n, j] = jnp.zeros_like(stage[n, j])

        pltpu.make_async_copy(stage.at[n], outs[r], away.at[n]).start()
    pltpu.make_async_copy(stay_ref, stay, stay_sem.at[0]).wait()
    pltpu.make_async_copy(stay, stay_ref, stay_sem.at[1]).start()
    for n, r in enumerate(SEND_ORDER):
        pltpu.make_async_copy(stage.at[n], outs[r], away.at[n]).wait()
    pltpu.make_async_copy(stay, stay_ref, stay_sem.at[1]).wait()


def local_part(z, late, first, patches, coarse):
    shape = (QUARTER + patches.shape[0] // NZ, patches.shape[1], PB, LANES)
    stay = (QUARTER, F, PB, LANES)
    return pl.pallas_call(
        local_kernel,
        out_shape=[jax.ShapeDtypeStruct(shape, BF16)] * NZ + [jax.ShapeDtypeStruct(stay, BF16)],
        in_specs=[SMEM, SMEM, SMEM, ANY, ANY],
        out_specs=[ANY] * (NZ + 1),
        scratch_shapes=[
            pltpu.VMEM((NZ, *shape), BF16),
            pltpu.VMEM(stay, BF16),
            pltpu.SemaphoreType.DMA((NZ,)),
            pltpu.SemaphoreType.DMA((NZ,)),
            pltpu.SemaphoreType.DMA((2,)),
        ],
        compiler_params=PARAMS,
        cost_estimate=cost(2**22),
    )(z, late, first, patches, coarse)


def merge_kernel(order_ref, pick_ref, received_ref, coarse_ref, after_ref, *rest):
    outs, (stage, into, away) = rest[:-3], rest[-3:]
    fields = pl.ds(0, EARLY)
    for n, r in enumerate(SEND_ORDER):
        for j in range(QUARTER):
            k = r * QUARTER + j
            box = pick_ref[k]

            @pl.when(box < 0)
            def _(n=n, j=j, k=k):
                pltpu.make_async_copy(received_ref.at[order_ref[k], fields], stage.at[n, j], into.at[n]).start()

            @pl.when(box >= 0)
            def _(n=n, j=j, box=box):
                pltpu.make_async_copy(coarse_ref.at[fields, box], stage.at[n, j], into.at[n]).start()

    stage_out(stage, [outs[r] for r in SEND_ORDER], into, away)


def merge(order, pick, received, coarse, after):
    shape = (QUARTER, EARLY, PB, LANES)
    return pl.pallas_call(
        merge_kernel,
        out_shape=[jax.ShapeDtypeStruct(shape, BF16)] * NZ,
        in_specs=[SMEM, SMEM, ANY, ANY, ANY],
        out_specs=[ANY] * NZ,
        scratch_shapes=[pltpu.VMEM((NZ, *shape), BF16)] + [pltpu.SemaphoreType.DMA((NZ,))] * 2,
        compiler_params=PARAMS,
        cost_estimate=cost(4 * 2**20),
    )(order, pick, received, coarse, after)


def output_kernel(slots_ref, out_ref, stage, into, away):
    ins = [pltpu.make_async_copy(slots_ref.at[:, f], stage.at[f], into.at[f]) for f in range(F)]
    outs = [pltpu.make_async_copy(stage.at[f], out_ref.at[f], away.at[f]) for f in range(F)]
    for copy in ins:
        copy.start()
    for copy, out in zip(ins, outs):
        copy.wait()
        out.start()
    for out in outs:
        out.wait()


def slot_output(slots):
    return pl.pallas_call(
        output_kernel,
        out_shape=jax.ShapeDtypeStruct((F, SLOTS, PB, LANES), BF16),
        in_specs=[ANY],
        out_specs=ANY,
        scratch_shapes=[pltpu.VMEM((F, SLOTS, PB, LANES), BF16)] + [pltpu.SemaphoreType.DMA((F,))] * 2,
        compiler_params=PARAMS,
        cost_estimate=cost(8 * 2**20),
    )(slots)


def gram_kernel(offset, has_before, scale, weight_ref, z_ref, x0, x1, x2, x3, *rest):
    f = pl.program_id(0)
    before_ref, out_ref, total = rest[0], rest[-1 if scale is None else -2], rest[-1]

    @pl.when(f == 0)
    def _():
        total[...] = before_ref[...] if has_before else jnp.zeros_like(total)

    cells = x0.shape[0] * PB
    wide = jnp.concatenate([x[...].reshape(cells, LANES) for x in (x0, x1, x2, x3)], axis=1)
    product = lax.dot_general(wide, wide, (((0,), (0,)), ((), ())), preferred_element_type=F32)
    for b in range(NZ):
        total[b] += weight_ref[offset + f] * product[:, b * LANES : (b + 1) * LANES]

    if scale is not None:

        @pl.when(f == pl.num_programs(0) - 1)
        def _():
            z = z_ref[0]
            rows = S // 128
            for a in range(NZ):
                ga = (GRAM_ORDER[a] + z) % NZ
                for b in range(NZ):
                    gb = (GRAM_ORDER[b] + z) % NZ
                    for i in range(rows):
                        part = total[b, pl.ds(a * LANES + i, LANES // rows, stride=rows), :]
                        start = ga * (LANES // rows) * 16 + gb * rows + i
                        out_ref[pl.ds(start, LANES // rows, stride=16), :] = part * scale


def gram(weight, z, xs, before=None, offset=0, scale=None, effort=1, after=None):
    boxes, fields = xs[0].shape[:2]
    block = pl.BlockSpec((boxes, 1, PB, LANES), lambda f: (0, f, 0, 0))
    whole = pl.BlockSpec((NZ, S, LANES), lambda f: (0, 0, 0))
    more = [] if before is None else [(before, whole)]
    if after is not None:
        more.append((after, ANY))
    last = scale is not None
    return pl.pallas_call(
        lambda *refs: gram_kernel(offset, before is not None, scale, *refs),
        grid=(fields,),
        out_shape=jax.ShapeDtypeStruct((S * NZ, LANES) if last else (NZ, S, LANES), F32),
        in_specs=[SMEM, SMEM] + [block] * NZ + [spec for _, spec in more],
        out_specs=pl.BlockSpec((S * NZ, LANES), lambda f: (0, 0)) if last else whole,
        scratch_shapes=[pltpu.VMEM((NZ, S, LANES), F32)] if last else [],
        compiler_params=PARAMS,
        cost_estimate=cost(effort * (fields * 2**20 + 2**21), effort * 2 * fields * boxes * PB * S * S),
    )(weight, z, *xs, *[x for x, _ in more])


def shift(x, by):
    return lax.ppermute(x, "snap", [(i, (i + by) % NZ) for i in range(NZ)])


def exchange(sends):
    return tuple(shift(sends[(NZ - g) % NZ], (NZ - g) % NZ) if g else sends[0] for g in GRAM_ORDER)


def anchor(*behind):
    def kernel(*refs):
        refs[-1][...] = jnp.zeros_like(refs[-1])

    return pl.pallas_call(
        kernel,
        out_shape=jax.ShapeDtypeStruct((8, LANES), F32),
        in_specs=[ANY] * len(behind),
        out_specs=VMEM,
        compiler_params=PARAMS,
        cost_estimate=cost(2**30, 2**40),
    )(*behind)


def on_device(coarse, fine_cells, patch_block, fine_map, field_weight):
    own = lax.axis_index(XY).astype(I32)
    z = lax.axis_index("snap").astype(I32)
    per_owner = fine_cells.shape[0]
    blocks_dev = coarse.shape[1] // PB
    coarse_boxes = coarse.reshape(F, blocks_dev, PB, LANES)
    first, slot, has_patch, order, pick, late = tables(patch_block, own, z, per_owner, blocks_dev)
    at_z = z.reshape(1)

    (across,) = gather_free(first, coarse_boxes, (2,), field_weight)
    outgoing, patches = restrict(slot, has_patch, fine_map, fine_cells, across)
    up, down = gather_free(first, coarse_boxes, (1, 3), patches)
    received = lax.all_to_all(outgoing, XY, split_axis=0, concat_axis=0, tiled=True)
    *local_sends, stay = local_part(at_z, late, first, patches, coarse_boxes)
    free = exchange((stay, up, across, down))
    local = exchange(local_sends)

    slots = exchange(merge(order, pick, received, coarse_boxes, anchor(free[1], local_sends[0])))
    total = gram(field_weight, at_z, free, effort=400)
    total = gram(field_weight, at_z, local, total, EARLY, effort=400)

    scale = 1.0 / (F * coarse.shape[1] * OWNERS)
    shares = gram(field_weight, at_z, slots, total, 0, scale)

    collected = lax.all_to_all(shares, ALL, split_axis=0, concat_axis=0, tiled=True)
    restricted = slot_output(received)
    summed = jnp.sum(collected.reshape(128, NZ, NZ, LANES), axis=0)
    gram_matrix = summed.transpose(1, 0, 2).reshape(S // 128, S)
    return (gram_matrix, restricted)


def solution(mesh):
    return jax.shard_map(
        on_device,
        mesh=mesh,
        in_specs=(
            P(None, ("tile", "level"), "snap"),
            P(("tile", "level"), None, None, "snap"),
            P(),
            P(),
            P(),
        ),
        out_specs=(P(("snap", "tile", "level"), None), P(None, ("tile", "level"), None, "snap")),
        check_vma=False,
    )
```

time: 179 us -> 146 us (0.82)
  waiting for transfers between devices: 89.8 us -> 66.3 us
  starting transfers between devices: 33.3 us -> 29.2 us
  Pallas kernels: 45.7 us -> 41.9 us
    ppermute x9, waiting for transfers between devices: 63.1 us -> 34.1 us  [shift(): return lax.ppermute(x, 'snap', [(i, (i + by) % NZ) for i in range(NZ)])]
    all_to_all x2 -> x1, starting transfers between devices: 16.6 us -> 8.11 us  [on_device(): lax.all_to_all(outgoing, XY, split_axis=0, concat_axis=0, tiled=True)]
    ppermute x9, starting transfers between devices: 7.08 us -> 12.7 us  [shift(): return lax.ppermute(x, 'snap', [(i, (i + by) % NZ) for i in range(NZ)])]
    all_to_all x2 -> x1, waiting for transfers between devices: 11.2 us -> 16.6 us  [on_device(): lax.all_to_all(outgoing, XY, split_axis=0, concat_axis=0, tiled=True)]
    pallas_call x2 -> x1, Pallas kernels: 12 us -> 8.64 us  [restrict(): pl.pallas_call(lambda *refs: restrict_kernel(steps, group, fields, *refs)...]
  transfers between devices with their start and end apart: 12 -> 11, of which waited for: 7 -> 9; matrix products, arithmetic and copies ran while one was open for 0% -> 2% of each run, Pallas kernels for 16% -> 24%
where the time goes in v2:
time: 146 us; the launch traced here: 145 us
  waiting for transfers between devices  66.3 us (45%)
  Pallas kernels  41.9 us (29%)
  starting transfers between devices  29.2 us (20%)
  other arithmetic  5.62 us (4%)
    ppermute x9, waiting for transfers between devices, shift(): return lax.ppermute(x, 'snap', [(i, (i + by) % NZ) for i in range(NZ)])  34.1 us
    all_to_all x1, waiting for transfers between devices, on_device(): lax.all_to_all(outgoing, XY, split_axis=0, concat_axis=0, tiled=True)  16.6 us
    all_to_all x1, waiting for transfers between devices, on_device(): lax.all_to_all(shares, ALL, split_axis=0, concat_axis=0, tiled=True)  15.6 us
    pallas_call x3, Pallas kernels, gram(): pl.pallas_call(lambda *refs: gram_kernel(offset, before is not None, scal...  15.2 us
    ppermute x9, starting transfers between devices, shift(): return lax.ppermute(x, 'snap', [(i, (i + by) % NZ) for i in range(NZ)])  12.7 us
    pallas_call x1, Pallas kernels, restrict(): pl.pallas_call(lambda *refs: restrict_kernel(steps, group, fields, *refs)...  8.64 us
    all_to_all x1, starting transfers between devices, on_device(): lax.all_to_all(shares, ALL, split_axis=0, concat_axis=0, tiled=True)  8.36 us
    all_to_all x1, starting transfers between devices, on_device(): lax.all_to_all(outgoing, XY, split_axis=0, concat_axis=0, tiled=True)  8.11 us
  transfers between devices with their start and end apart: 11, of which 9 were waited for; matrix products, arithmetic and copies ran while one was open for 2% of the time, Pallas kernels for 24%

profile of v2, /device:TPU:1, one launch (start us, length us, event | category | flops | bytes accessed | tf_op | source)
XLA Modules:
  0.0 145.0 jit_solution(5470228722008393654)
XLA Ops:
  3.6 3.0 %shard_map.68.refs_4_ = bf16[16,4,64,128]{3,2,1,0:T(8,128)(2,1)} custom-call(s32[64]{0:T(128)} %get-tuple-element.29.refs_0_.first_ref, bf16[4,128,64,128]{3,2,1,0:T(8,128)(2,1)} %bitcast.9, f32[4]{0:T(128)} %refs_0_.5), custom_call_target="tpu_custom_call" | custom-call | bytes 2097152 | tf_op jit(solution)/shard_map/pallas_call | solution.py:77
  6.6 4.5 %collective-permute-start = (bf16[16,4,64,128]{3,2,1,0:T(8,128)(2,1)}, bf16[16,4,64,128]{3,2,1,0:T(8,128)(2,1)S(1)}, u32[]{:S(2)}, u32[]{:S(2)}) collective-permute-start(bf16[16,4,64,128]{3,2,1,0:T(8,128)(2,1)} %shard_map.68.refs_4_), channel_id=1, source_target_pairs={{0,64},{32,96},{64,0},{96,32},{1,65},{33,97},{65,1},{97,33},{2,66}... | collective-permute-start | bytes 3145736 | tf_op jit(solution)/shard_map/ppermute | solution.py:304
  12.0 8.6 %shard_map.69 = (bf16[64,4,64,128]{3,2,1,0:T(8,128)(2,1)}, bf16[24,2,64,128]{3,2,1,0:T(8,128)(2,1)}) custom-call(s32[24]{0:T(128)} %copy-done, s32[64]{0:T(128)} %convert_element_type.23.refs_1_, s32[1,512]{1,0:T(1,128)} %bitcast.15, bf16[24,4,512,128]{3,2,1,0:T(8,128)(2,1)} %refs_3_.1, bf16[16,4,64,128]{3,2,1,0:T(8,128)(2,1)} %shard_map.68.refs_4_), custom_call_target="tpu_custom_call" | custom-call | flops 805306368 | bytes 16777216 | tf_op jit(solution)/shard_map/pallas_call | solution.py:123
  20.7 8.1 %all-to-all-start = ((bf16[64,4,64,128]{3,2,1,0:T(8,128)(2,1)}), bf16[64,4,64,128]{3,2,1,0:T(8,128)(2,1)}, u32[]{:S(2)}, u32[]{:S(2)}) async-start(bf16[64,4,64,128]{3,2,1,0:T(8,128)(2,1)} %get-tuple-element.15), calls=%async_computation | async-start | bytes 8388608 | tf_op jit(solution)/shard_map/all_to_all | solution.py:337
  28.8 3.4 %shard_map.73 = (bf16[16,4,64,128]{3,2,1,0:T(8,128)(2,1)}, bf16[16,4,64,128]{3,2,1,0:T(8,128)(2,1)}) custom-call(s32[64]{0:T(128)} %get-tuple-element.29.refs_0_.first_ref, bf16[4,128,64,128]{3,2,1,0:T(8,128)(2,1)} %bitcast.10, bf16[24,2,64,128]{3,2,1,0:T(8,128)(2,1)} %get-tuple-element.16.patches_ref.refs_2_), custom_call_target="tpu_custom_call" | custom-call | bytes 4194304 | tf_op jit(solution)/shard_map/pallas_call | solution.py:77
  32.7 1.0 collective-permute-start.8
  34.3 4.7 %shard_map.70 = (bf16[22,2,64,128]{3,2,1,0:T(8,128)(2,1)}, bf16[22,2,64,128]{3,2,1,0:T(8,128)(2,1)}, bf16[22,2,64,128]{3,2,1,0:T(8,128)(2,1)}, bf16[22,2,64,128]{3,2,1,0:T(8,128)(2,1)}, bf16[16,4,64,128]{3,2,1,0:T(8,128)(2,1)}) custom-call(s32[1]{0:T(128)} %bitcast.z_ref.refs_1_, s32[64]{0:T(128)} %broadcast_add_fusion.2.late_ref, ...), custom_call_target="tpu_custom_call" | custom-call | bytes 4194304 | tf_op jit(solution)/shard_map/pallas_call | solution.py:180
  38.9 1.3 collective-permute-start.4
  40.2 2.1 %collective-permute-start.5 = (bf16[22,2,64,128]{3,2,1,0:T(8,128)(2,1)}, bf16[22,2,64,128]{3,2,1,0:T(8,128)(2,1)}, u32[]{:S(2)}, u32[]{:S(2)}) collective-permute-start(bf16[22,2,64,128]{3,2,1,0:T(8,128)(2,1)} %get-tuple-element.23), channel_id=1, source_target_pairs={{0,96},{32,0},{64,32},{96,64},{1,97},{33,1},{65,33},{97,65},{2,98}... | collective-permute-start | bytes 2162696 | tf_op jit(solution)/shard_map/ppermute | solution.py:304
  43.1 1.0 copy-done.2
  44.7 13.1 %collective-permute-done.7.refs_4_ = bf16[16,4,64,128]{3,2,1,0:T(8,128)(2,1)} collective-permute-done((bf16[16,4,64,128]{3,2,1,0:T(8,128)(2,1)}, bf16[16,4,64,128]{3,2,1,0:T(8,128)(2,1)}, u32[]{:S(2)}, u32[]{:S(2)}) %collective-permute-start.7) | collective-permute-done | bytes 1048608 | tf_op jit(solution)/shard_map/ppermute | solution.py:304
  58.6 5.8 %shard_map.74.refs_6_ = f32[4,512,128]{2,1,0:T(8,128)} custom-call(f32[4]{0:T(128)} %refs_0_.5, s32[1]{0:T(128)} %bitcast.z_ref.refs_1_, bf16[16,4,64,128]{3,2,1,0:T(8,128)(2,1)} %get-tuple-element.25.refs_2_, bf16[16,4,64,128]{3,2,1,0:T(8,128)(2,1)} %copy-done.2, bf16[16,4,64,128]{3,2,1,0:T(8,128)(2,1)} %collective-permute-done.7.refs_4_, ...), custom_call_target="tpu_custom_call" | custom-call | flops 858993459200 | bytes 2516582400 | tf_op jit(solution)/shard_map/pallas_call | solution.py:291
  64.4 16.6 %all-to-all-done.received_ref.slots_ref = bf16[64,4,64,128]{3,2,1,0:T(8,128)(2,1)} async-done(((bf16[64,4,64,128]{3,2,1,0:T(8,128)(2,1)}), bf16[64,4,64,128]{3,2,1,0:T(8,128)(2,1)}, u32[]{:S(2)}, u32[]{:S(2)}) %all-to-all-start) | async-done | bytes 4194336 | tf_op jit(solution)/shard_map/all_to_all | solution.py:337
  81.0 3.1 %shard_map.72 = (bf16[16,2,64,128]{3,2,1,0:T(8,128)(2,1)}, bf16[16,2,64,128]{3,2,1,0:T(8,128)(2,1)}, bf16[16,2,64,128]{3,2,1,0:T(8,128)(2,1)}, bf16[16,2,64,128]{3,2,1,0:T(8,128)(2,1)}) custom-call(s32[64]{0:T(128)} %copy-done.1, s32[64]{0:T(128)} %broadcast_select_fusion.1.pick_ref, bf16[64,4,64,128]{3,2,1,0:T(8,128)(2,1)} %all-to-all-done.received_ref.slots_ref, ...), custom_call_target="tpu_custom_call" | custom-call | bytes 4194304 | tf_op jit(solution)/shard_map/pallas_call | solution.py:218
  84.2 3.1 %collective-permute-start.2 = (bf16[16,2,64,128]{3,2,1,0:T(8,128)(2,1)}, bf16[16,2,64,128]{3,2,1,0:T(8,128)(2,1)}, u32[]{:S(2)}, u32[]{:S(2)}) collective-permute-start(bf16[16,2,64,128]{3,2,1,0:T(8,128)(2,1)} %get-tuple-element.20), channel_id=1, source_target_pairs={{0,96},{32,0},{64,32},{96,64},{1,97},{33,1},{65,33},{97,65},{2,98}... | collective-permute-start | bytes 1572872 | tf_op jit(solution)/shard_map/ppermute | solution.py:304
  87.3 1.4 collective-permute-done.5.refs_4_
  89.4 4.8 %shard_map.75.refs_6_ = f32[4,512,128]{2,1,0:T(8,128)} custom-call(f32[4]{0:T(128)} %refs_0_.5, s32[1]{0:T(128)} %bitcast.z_ref.refs_1_, bf16[22,2,64,128]{3,2,1,0:T(8,128)(2,1)} %get-tuple-element.17.refs_1_.refs_2_, bf16[22,2,64,128]{3,2,1,0:T(8,128)(2,1)} %collective-permute-done.4.refs_3_, bf16[22,2,64,128]{3,2,1,0:T(8,128)(2,1)} %collective-permute-done.5.refs_4_, ...), custom_call_target="tpu_custom_call" | custom-call | flops 590558003200 | bytes 1677721600 | tf_op jit(solution)/shard_map/pallas_call | solution.py:291
  94.2 6.1 %collective-permute-done.1.refs_3_ = bf16[16,2,64,128]{3,2,1,0:T(8,128)(2,1)} collective-permute-done((bf16[16,2,64,128]{3,2,1,0:T(8,128)(2,1)}, bf16[16,2,64,128]{3,2,1,0:T(8,128)(2,1)}, u32[]{:S(2)}, u32[]{:S(2)}) %collective-permute-start.1) | collective-permute-done | bytes 524320 | tf_op jit(solution)/shard_map/ppermute | solution.py:304
  100.3 11.0 %collective-permute-done.2.refs_4_ = bf16[16,2,64,128]{3,2,1,0:T(8,128)(2,1)} collective-permute-done((bf16[16,2,64,128]{3,2,1,0:T(8,128)(2,1)}, bf16[16,2,64,128]{3,2,1,0:T(8,128)(2,1)}, u32[]{:S(2)}, u32[]{:S(2)}) %collective-permute-start.2) | collective-permute-done | bytes 524320 | tf_op jit(solution)/shard_map/ppermute | solution.py:304
  111.3 1.1 collective-permute-done.3.refs_5_
  112.4 4.6 %shard_map.76 = f32[2048,128]{1,0:T(8,128)} custom-call(f32[4]{0:T(128)} %refs_0_.5, s32[1]{0:T(128)} %bitcast.z_ref.refs_1_, bf16[16,2,64,128]{3,2,1,0:T(8,128)(2,1)} %get-tuple-element.18.refs_2_, bf16[16,2,64,128]{3,2,1,0:T(8,128)(2,1)} %collective-permute-done.1.refs_3_, bf16[16,2,64,128]{3,2,1,0:T(8,128)(2,1)} %collective-permute-done.2.refs_4_, ...), custom_call_target="tpu_custom_call" | custom-call | flops 1073741824 | bytes 4194304 | tf_op jit(solution)/shard_map/pallas_call | solution.py:291
  117.0 8.4 %all-to-all-start.1 = ((f32[128,16,128]{2,1,0:T(8,128)}), f32[128,16,128]{2,1,0:T(8,128)S(1)}, u32[]{:S(2)}, u32[]{:S(2)}) async-start(f32[128,16,128]{2,1,0:T(8,128)} %bitcast.13), calls=%async_computation.1 | async-start | bytes 2097152 | tf_op jit(solution)/shard_map/all_to_all | solution.py:349
  125.4 3.3 %shard_map.77 = bf16[4,64,64,128]{3,2,1,0:T(8,128)(2,1)} custom-call(bf16[64,4,64,128]{3,2,1,0:T(8,128)(2,1)} %all-to-all-done.received_ref.slots_ref), custom_call_target="tpu_custom_call" | custom-call | bytes 8388608 | tf_op jit(solution)/shard_map/pallas_call | solution.py:242
  128.7 15.6 %all-to-all-done.1 = f32[128,16,128]{2,1,0:T(8,128)S(1)} async-done(((f32[128,16,128]{2,1,0:T(8,128)}), f32[128,16,128]{2,1,0:T(8,128)S(1)}, u32[]{:S(2)}, u32[]{:S(2)}) %all-to-all-start.1) | async-done | bytes 1048608 | tf_op jit(solution)/shard_map/all_to_all | solution.py:349
  (37 shorter events, 8.6 us)
Async XLA Ops:
  0.7 41.7 %copy-start.1 = (s32[64]{0:T(128)}, s32[64]{0:T(128)S(1)}, u32[]{:S(2)}) copy-start(s32[64]{0:T(128)S(1)} %get-tuple-element.33.order_ref) | copy-start | bytes 772
  6.6 36.6 %collective-permute-start = (bf16[16,4,64,128]{3,2,1,0:T(8,128)(2,1)}, bf16[16,4,64,128]{3,2,1,0:T(8,128)(2,1)S(1)}, u32[]{:S(2)}, u32[]{:S(2)}) collective-permute-start(bf16[16,4,64,128]{3,2,1,0:T(8,128)(2,1)} %shard_map.68.refs_4_), channel_id=1, source_target_pairs={{0,64},{32,96},{64,0},{96,32},{1,65},{33,97},{65,1},{97,33},{2,66}... | collective-permute-start | bytes 3145736 | tf_op jit(solution)/shard_map/ppermute | solution.py:304
  11.4 0.6 copy-start
  20.7 60.3 %all-to-all-start = ((bf16[64,4,64,128]{3,2,1,0:T(8,128)(2,1)}), bf16[64,4,64,128]{3,2,1,0:T(8,128)(2,1)}, u32[]{:S(2)}, u32[]{:S(2)}) async-start(bf16[64,4,64,128]{3,2,1,0:T(8,128)(2,1)} %get-tuple-element.15), calls=%async_computation | async-start | bytes 8388608 | tf_op jit(solution)/shard_map/all_to_all | solution.py:337
  32.2 25.6 %collective-permute-start.7 = (bf16[16,4,64,128]{3,2,1,0:T(8,128)(2,1)}, bf16[16,4,64,128]{3,2,1,0:T(8,128)(2,1)}, u32[]{:S(2)}, u32[]{:S(2)}) collective-permute-start(bf16[16,4,64,128]{3,2,1,0:T(8,128)(2,1)} %get-tuple-element.26), channel_id=1, source_target_pairs={{0,96},{32,0},{64,32},{96,64},{1,97},{33,1},{65,33},{97,65},{2,98}... | collective-permute-start | bytes 3145736 | tf_op jit(solution)/shard_map/ppermute | solution.py:304
  32.7 25.9 %collective-permute-start.8 = (bf16[16,4,64,128]{3,2,1,0:T(8,128)(2,1)}, bf16[16,4,64,128]{3,2,1,0:T(8,128)(2,1)}, u32[]{:S(2)}, u32[]{:S(2)}) collective-permute-start(bf16[16,4,64,128]{3,2,1,0:T(8,128)(2,1)} %get-tuple-element.27), channel_id=1, source_target_pairs={{0,32},{32,64},{64,96},{96,0},{1,33},{33,65},{65,97},{97,1},{2,34}... | collective-permute-start | bytes 3145736 | tf_op jit(solution)/shard_map/ppermute | solution.py:304
  38.9 48.4 %collective-permute-start.4 = (bf16[22,2,64,128]{3,2,1,0:T(8,128)(2,1)}, bf16[22,2,64,128]{3,2,1,0:T(8,128)(2,1)}, u32[]{:S(2)}, u32[]{:S(2)}) collective-permute-start(bf16[22,2,64,128]{3,2,1,0:T(8,128)(2,1)} %get-tuple-element.22), channel_id=1, source_target_pairs={{0,64},{32,96},{64,0},{96,32},{1,65},{33,97},{65,1},{97,33},{2,66}... | collective-permute-start | bytes 2162696 | tf_op jit(solution)/shard_map/ppermute | solution.py:304
  40.2 48.5 %collective-permute-start.5 = (bf16[22,2,64,128]{3,2,1,0:T(8,128)(2,1)}, bf16[22,2,64,128]{3,2,1,0:T(8,128)(2,1)}, u32[]{:S(2)}, u32[]{:S(2)}) collective-permute-start(bf16[22,2,64,128]{3,2,1,0:T(8,128)(2,1)} %get-tuple-element.23), channel_id=1, source_target_pairs={{0,96},{32,0},{64,32},{96,64},{1,97},{33,1},{65,33},{97,65},{2,98}... | collective-permute-start | bytes 2162696 | tf_op jit(solution)/shard_map/ppermute | solution.py:304
  43.1 1.0 copy-start.2
  43.1 46.3 %collective-permute-start.6 = (bf16[22,2,64,128]{3,2,1,0:T(8,128)(2,1)}, bf16[22,2,64,128]{3,2,1,0:T(8,128)(2,1)}, u32[]{:S(2)}, u32[]{:S(2)}) collective-permute-start(bf16[22,2,64,128]{3,2,1,0:T(8,128)(2,1)} %get-tuple-element.24), channel_id=1, source_target_pairs={{0,32},{32,64},{64,96},{96,0},{1,33},{33,65},{65,97},{97,1},{2,34}... | collective-permute-start | bytes 2162696 | tf_op jit(solution)/shard_map/ppermute | solution.py:304
  84.1 16.1 %collective-permute-start.1 = (bf16[16,2,64,128]{3,2,1,0:T(8,128)(2,1)}, bf16[16,2,64,128]{3,2,1,0:T(8,128)(2,1)}, u32[]{:S(2)}, u32[]{:S(2)}) collective-permute-start(bf16[16,2,64,128]{3,2,1,0:T(8,128)(2,1)} %get-tuple-element.19), channel_id=1, source_target_pairs={{0,64},{32,96},{64,0},{96,32},{1,65},{33,97},{65,1},{97,33},{2,66}... | collective-permute-start | bytes 1572872 | tf_op jit(solution)/shard_map/ppermute | solution.py:304
  84.2 27.0 %collective-permute-start.2 = (bf16[16,2,64,128]{3,2,1,0:T(8,128)(2,1)}, bf16[16,2,64,128]{3,2,1,0:T(8,128)(2,1)}, u32[]{:S(2)}, u32[]{:S(2)}) collective-permute-start(bf16[16,2,64,128]{3,2,1,0:T(8,128)(2,1)} %get-tuple-element.20), channel_id=1, source_target_pairs={{0,96},{32,0},{64,32},{96,64},{1,97},{33,1},{65,33},{97,65},{2,98}... | collective-permute-start | bytes 1572872 | tf_op jit(solution)/shard_map/ppermute | solution.py:304
  87.3 25.0 %collective-permute-start.3 = (bf16[16,2,64,128]{3,2,1,0:T(8,128)(2,1)}, bf16[16,2,64,128]{3,2,1,0:T(8,128)(2,1)}, u32[]{:S(2)}, u32[]{:S(2)}) collective-permute-start(bf16[16,2,64,128]{3,2,1,0:T(8,128)(2,1)} %get-tuple-element.21), channel_id=1, source_target_pairs={{0,32},{32,64},{64,96},{96,0},{1,33},{33,65},{65,97},{97,1},{2,34}... | collective-permute-start | bytes 1572872 | tf_op jit(solution)/shard_map/ppermute | solution.py:304
  117.0 27.3 %all-to-all-start.1 = ((f32[128,16,128]{2,1,0:T(8,128)}), f32[128,16,128]{2,1,0:T(8,128)S(1)}, u32[]{:S(2)}, u32[]{:S(2)}) async-start(f32[128,16,128]{2,1,0:T(8,128)} %bitcast.13), calls=%async_computation.1 | async-start | bytes 2097152 | tf_op jit(solution)/shard_map/all_to_all | solution.py:349

commit v3 on v2

--- a/solution.py
+++ b/solution.py
@@ -29,7 +29,7 @@
     return pl.CostEstimate(flops=flops, bytes_accessed=bytes_accessed, transcendentals=0)
 
 
-def tables(patch_block, own, z, per_owner, blocks_dev):
+def free_boxes(patch_block, own, z, blocks_dev):
     k = jnp.arange(SLOTS, dtype=I32)
     order = QUARTER * ((z + k // QUARTER) % NZ) + k % QUARTER
     boxes = jnp.arange(blocks_dev, dtype=I32)
@@ -38,7 +38,12 @@
     rank_free = jnp.sum((free[None, :] & (boxes[None, :] < boxes[:, None])).astype(I32), axis=1)
     place = jnp.where(free, rank_free, -1)
     first = jnp.sum(jnp.where(place[None, :] == order[:, None], boxes[None, :], 0), axis=1)
-
+    return order, place, first
+
+
+def tables(patch_block, own, order, place, per_owner, blocks_dev):
+    k = jnp.arange(SLOTS, dtype=I32)
+    boxes = jnp.arange(blocks_dev, dtype=I32)
     target = lax.shift_right_logical(patch_block, jnp.int32(blocks_dev.bit_length() - 1))
     own_target = lax.dynamic_slice_in_dim(target, own * per_owner, per_owner)
     p = jnp.arange(per_owner, dtype=I32)
@@ -53,7 +58,7 @@
     filled_at = jnp.any(filled[None, :] & (k[None, :] == order[:, None]), axis=1)
     pick = jnp.where(filled_at, -1, second)
     late = jnp.sum(jnp.where(place[None, :] == SLOTS + order[:, None], boxes[None, :] + 1, 0), axis=1) - 1
-    return first, slot, has_patch, order, pick, late
+    return slot, has_patch, pick, late
 
 
 def stage_out(stage, outs, into, away):
@@ -250,9 +255,9 @@
     )(slots)
 
 
-def gram_kernel(offset, has_before, scale, weight_ref, z_ref, x0, x1, x2, x3, *rest):
+def gram_kernel(offset, has_before, scale, weight_ref, place_ref, x0, x1, x2, x3, *rest):
     f = pl.program_id(0)
-    before_ref, out_ref, total = rest[0], rest[-1 if scale is None else -2], rest[-1]
+    before_ref, total = rest[0], rest[-1]
 
     @pl.when(f == 0)
     def _():
@@ -268,19 +273,29 @@
 
         @pl.when(f == pl.num_programs(0) - 1)
         def _():
-            z = z_ref[0]
-            rows = S // 128
-            for a in range(NZ):
-                ga = (GRAM_ORDER[a] + z) % NZ
-                for b in range(NZ):
-                    gb = (GRAM_ORDER[b] + z) % NZ
-                    for i in range(rows):
-                        part = total[b, pl.ds(a * LANES + i, LANES // rows, stride=rows), :]
-                        start = ga * (LANES // rows) * 16 + gb * rows + i
-                        out_ref[pl.ds(start, LANES // rows, stride=16), :] = part * scale
-
-
-def gram(weight, z, xs, before=None, offset=0, scale=None, effort=1, after=None):
+            for level in range(2):
+
+                @pl.when(place_ref[1] == level)
+                def _(level=level):
+                    split_pieces(place_ref[0], total, scale, rest[-3], rest[-2], level)
+
+
+def split_pieces(z, total, scale, keep_ref, send_ref, level):
+    rows = 4
+    per_group = LANES // (2 * rows)
+    for a in range(NZ):
+        ga = (GRAM_ORDER[a] + z) % NZ
+        for b in range(NZ):
+            gb = (GRAM_ORDER[b] + z) % NZ
+            for half in range(2):
+                out_ref = keep_ref if half == level else send_ref
+                for i in range(rows):
+                    part = total[b, pl.ds(a * LANES + half * rows + i, per_group, stride=2 * rows), :]
+                    start = ga * per_group * NZ * rows + gb * rows + i
+                    out_ref[pl.ds(start, per_group, stride=NZ * rows), :] = part * scale
+
+
+def gram(weight, place, xs, before=None, offset=0, scale=None, effort=1, after=None):
     boxes, fields = xs[0].shape[:2]
     block = pl.BlockSpec((boxes, 1, PB, LANES), lambda f: (0, f, 0, 0))
     whole = pl.BlockSpec((NZ, S, LANES), lambda f: (0, 0, 0))
@@ -291,13 +306,13 @@
     return pl.pallas_call(
         lambda *refs: gram_kernel(offset, before is not None, scale, *refs),
         grid=(fields,),
-        out_shape=jax.ShapeDtypeStruct((S * NZ, LANES) if last else (NZ, S, LANES), F32),
+        out_shape=[jax.ShapeDtypeStruct((S * NZ // 2, LANES), F32)] * 2 if last else jax.ShapeDtypeStruct((NZ, S, LANES), F32),
         in_specs=[SMEM, SMEM] + [block] * NZ + [spec for _, spec in more],
-        out_specs=pl.BlockSpec((S * NZ, LANES), lambda f: (0, 0)) if last else whole,
+        out_specs=[pl.BlockSpec((S * NZ // 2, LANES), lambda f: (0, 0))] * 2 if last else whole,
         scratch_shapes=[pltpu.VMEM((NZ, S, LANES), F32)] if last else [],
         compiler_params=PARAMS,
         cost_estimate=cost(effort * (fields * 2**20 + 2**21), effort * 2 * fields * boxes * PB * S * S),
-    )(weight, z, *xs, *[x for x, _ in more])
+    )(weight, place, *xs, *[x for x, _ in more])
 
 
 def shift(x, by):
@@ -328,10 +343,13 @@
     per_owner = fine_cells.shape[0]
     blocks_dev = coarse.shape[1] // PB
     coarse_boxes = coarse.reshape(F, blocks_dev, PB, LANES)
-    first, slot, has_patch, order, pick, late = tables(patch_block, own, z, per_owner, blocks_dev)
+    order, place, first = free_boxes(patch_block, own, z, blocks_dev)
     at_z = z.reshape(1)
+    spot = jnp.stack([z, lax.axis_index("level").astype(I32)])
 
     (across,) = gather_free(first, coarse_boxes, (2,), field_weight)
+    patch_block, across = lax.optimization_barrier((patch_block, across))
+    slot, has_patch, pick, late = tables(patch_block, own, order, place, per_owner, blocks_dev)
     outgoing, patches = restrict(slot, has_patch, fine_map, fine_cells, across)
     up, down = gather_free(first, coarse_boxes, (1, 3), patches)
     received = lax.all_to_all(outgoing, XY, split_axis=0, concat_axis=0, tiled=True)
@@ -340,15 +358,16 @@
     local = exchange(local_sends)
 
     slots = exchange(merge(order, pick, received, coarse_boxes, anchor(free[1], local_sends[0])))
-    total = gram(field_weight, at_z, free, effort=400)
-    total = gram(field_weight, at_z, local, total, EARLY, effort=400)
+    total = gram(field_weight, spot, free, effort=400)
+    total = gram(field_weight, spot, local, total, EARLY, effort=400)
 
     scale = 1.0 / (F * coarse.shape[1] * OWNERS)
-    shares = gram(field_weight, at_z, slots, total, 0, scale)
-
-    collected = lax.all_to_all(shares, ALL, split_axis=0, concat_axis=0, tiled=True)
+    keep, send = gram(field_weight, spot, slots, total, 0, scale)
+
+    shares = keep + lax.ppermute(send, "level", [(0, 1), (1, 0)])
+    collected = lax.all_to_all(shares, ("snap", "tile"), split_axis=0, concat_axis=0, tiled=True)
     restricted = slot_output(received)
-    summed = jnp.sum(collected.reshape(128, NZ, NZ, LANES), axis=0)
+    summed = jnp.sum(collected.reshape(S // 8, NZ, NZ, LANES), axis=0)
     gram_matrix = summed.transpose(1, 0, 2).reshape(S // 128, S)
     return (gram_matrix, restricted)
 

time: 146 us -> 143 us (0.979)
  waiting for transfers between devices: 66.3 us -> 60.3 us
  other arithmetic: 5.62 us -> 7.57 us
    all_to_all x1, waiting for transfers between devices: 15.6 us -> 8.91 us  [on_device(): lax.all_to_all(shares, ('snap', 'tile'), split_axis=0, concat_axis=0, til...]
    add x1 -> x2, other arithmetic: 0.01 us -> 1.94 us  [the longest x1 1.93 us: on_device(): shares = keep + lax.ppermute(send, 'level', [(0, 1), (1, 0)])]
    ppermute x0 -> x1, waiting for transfers between devices: none -> 1.75 us  [on_device(): shares = keep + lax.ppermute(send, 'level', [(0, 1), (1, 0)])]
  transfers between devices with their start and end apart: 11 -> 12, of which waited for: 9 -> 10; matrix products, arithmetic and copies ran while one was open for 2% -> 3% of each run, Pallas kernels for 24% -> 24%
where the time goes in v3:
time: 143 us; the launch traced here: 142 us
  waiting for transfers between devices  60.3 us (42%)
  Pallas kernels  42 us (29%)
  starting transfers between devices  30.1 us (21%)
  other arithmetic  7.57 us (5%)
    ppermute x9, waiting for transfers between devices, shift(): return lax.ppermute(x, 'snap', [(i, (i + by) % NZ) for i in range(NZ)])  33.1 us
    all_to_all x1, waiting for transfers between devices, on_device(): lax.all_to_all(outgoing, XY, split_axis=0, concat_axis=0, tiled=True)  16.6 us
    pallas_call x3, Pallas kernels, gram(): pl.pallas_call(lambda *refs: gram_kernel(offset, before is not None, scal...  15.3 us
    ppermute x9, starting transfers between devices, shift(): return lax.ppermute(x, 'snap', [(i, (i + by) % NZ) for i in range(NZ)])  12.4 us
    all_to_all x1, waiting for transfers between devices, on_device(): lax.all_to_all(shares, ('snap', 'tile'), split_axis=0, concat_axis=0, til...  8.91 us
    all_to_all x1, starting transfers between devices, on_device(): lax.all_to_all(shares, ('snap', 'tile'), split_axis=0, concat_axis=0, til...  8.72 us
    pallas_call x1, Pallas kernels, restrict(): pl.pallas_call(lambda *refs: restrict_kernel(steps, group, fields, *refs)...  8.63 us
    all_to_all x1, starting transfers between devices, on_device(): lax.all_to_all(outgoing, XY, split_axis=0, concat_axis=0, tiled=True)  8.11 us
  transfers between devices with their start and end apart: 12, of which 10 were waited for; matrix products, arithmetic and copies ran while one was open for 3% of the time, Pallas kernels for 24%

profile of v3, /device:TPU:1, one launch (start us, length us, event | category | flops | bytes accessed | tf_op | source)
XLA Modules:
  0.0 142.0 jit_solution(5134533561056943977)
XLA Ops:
  2.3 3.2 %shard_map.68.refs_4_ = bf16[16,4,64,128]{3,2,1,0:T(8,128)(2,1)} custom-call(s32[64]{0:T(128)} %select_reduce_fusion.2.refs_0_.first_ref, bf16[4,128,64,128]{3,2,1,0:T(8,128)(2,1)} %bitcast.10, f32[4]{0:T(128)} %refs_0_.5), custom_call_target="tpu_custom_call" | custom-call | bytes 2097152 | tf_op jit(solution)/shard_map/pallas_call | solution.py:82
  5.5 4.5 %collective-permute-start = (bf16[16,4,64,128]{3,2,1,0:T(8,128)(2,1)}, bf16[16,4,64,128]{3,2,1,0:T(8,128)(2,1)S(1)}, u32[]{:S(2)}, u32[]{:S(2)}) collective-permute-start(bf16[16,4,64,128]{3,2,1,0:T(8,128)(2,1)} %shard_map.68.refs_4_), channel_id=1, source_target_pairs={{0,64},{32,96},{64,0},{96,32},{1,65},{33,97},{65,1},{97,33},{2,66}... | collective-permute-start | bytes 3145736 | tf_op jit(solution)/shard_map/ppermute | solution.py:319
  11.1 8.6 %shard_map.69 = (bf16[64,4,64,128]{3,2,1,0:T(8,128)(2,1)}, bf16[24,2,64,128]{3,2,1,0:T(8,128)(2,1)}) custom-call(s32[24]{0:T(128)} %copy-done.1, s32[64]{0:T(128)} %convert_element_type.23.refs_1_, s32[1,512]{1,0:T(1,128)} %bitcast.15, bf16[24,4,512,128]{3,2,1,0:T(8,128)(2,1)} %refs_3_.1, bf16[16,4,64,128]{3,2,1,0:T(8,128)(2,1)} %shard_map.68.refs_4_), custom_call_target="tpu_custom_call" | custom-call | flops 805306368 | bytes 16777216 | tf_op jit(solution)/shard_map/pallas_call | solution.py:128
  19.7 8.1 %all-to-all-start = ((bf16[64,4,64,128]{3,2,1,0:T(8,128)(2,1)}), bf16[64,4,64,128]{3,2,1,0:T(8,128)(2,1)}, u32[]{:S(2)}, u32[]{:S(2)}) async-start(bf16[64,4,64,128]{3,2,1,0:T(8,128)(2,1)} %get-tuple-element.21), calls=%async_computation | async-start | bytes 8388608 | tf_op jit(solution)/shard_map/all_to_all | solution.py:355
  27.8 3.3 %shard_map.73 = (bf16[16,4,64,128]{3,2,1,0:T(8,128)(2,1)}, bf16[16,4,64,128]{3,2,1,0:T(8,128)(2,1)}) custom-call(s32[64]{0:T(128)} %select_reduce_fusion.2.refs_0_.first_ref, bf16[4,128,64,128]{3,2,1,0:T(8,128)(2,1)} %bitcast.11, bf16[24,2,64,128]{3,2,1,0:T(8,128)(2,1)} %get-tuple-element.22.patches_ref.refs_2_), custom_call_target="tpu_custom_call" | custom-call | bytes 4194304 | tf_op jit(solution)/shard_map/pallas_call | solution.py:82
  34.0 4.6 %shard_map.70 = (bf16[22,2,64,128]{3,2,1,0:T(8,128)(2,1)}, bf16[22,2,64,128]{3,2,1,0:T(8,128)(2,1)}, bf16[22,2,64,128]{3,2,1,0:T(8,128)(2,1)}, bf16[22,2,64,128]{3,2,1,0:T(8,128)(2,1)}, bf16[16,4,64,128]{3,2,1,0:T(8,128)(2,1)}) custom-call(s32[1]{0:T(128)} %bitcast.z_ref, s32[64]{0:T(128)} %broadcast_add_fusion.2.late_ref, ...), custom_call_target="tpu_custom_call" | custom-call | bytes 4194304 | tf_op jit(solution)/shard_map/pallas_call | solution.py:185
  38.6 1.1 collective-permute-start.4
  39.6 2.1 %collective-permute-start.5 = (bf16[22,2,64,128]{3,2,1,0:T(8,128)(2,1)}, bf16[22,2,64,128]{3,2,1,0:T(8,128)(2,1)}, u32[]{:S(2)}, u32[]{:S(2)}) collective-permute-start(bf16[22,2,64,128]{3,2,1,0:T(8,128)(2,1)} %get-tuple-element.29), channel_id=1, source_target_pairs={{0,96},{32,0},{64,32},{96,64},{1,97},{33,1},{65,33},{97,65},{2,98}... | collective-permute-start | bytes 2162696 | tf_op jit(solution)/shard_map/ppermute | solution.py:319
  44.7 12.1 %collective-permute-done.7.refs_4_ = bf16[16,4,64,128]{3,2,1,0:T(8,128)(2,1)} collective-permute-done((bf16[16,4,64,128]{3,2,1,0:T(8,128)(2,1)}, bf16[16,4,64,128]{3,2,1,0:T(8,128)(2,1)}, u32[]{:S(2)}, u32[]{:S(2)}) %collective-permute-start.7) | collective-permute-done | bytes 1048608 | tf_op jit(solution)/shard_map/ppermute | solution.py:319
  57.5 5.9 %shard_map.74.refs_6_ = f32[4,512,128]{2,1,0:T(8,128)} custom-call(f32[4]{0:T(128)} %refs_0_.5, s32[2]{0:T(128)} %pad_add_fusion.refs_1_, bf16[16,4,64,128]{3,2,1,0:T(8,128)(2,1)} %get-tuple-element.31.refs_2_, bf16[16,4,64,128]{3,2,1,0:T(8,128)(2,1)} %copy-done.3, bf16[16,4,64,128]{3,2,1,0:T(8,128)(2,1)} %collective-permute-done.7.refs_4_, ...), custom_call_target="tpu_custom_call" | custom-call | flops 858993459200 | bytes 2516582400 | tf_op jit(solution)/shard_map/pallas_call | solution.py:306
  63.5 16.6 %all-to-all-done.received_ref.slots_ref = bf16[64,4,64,128]{3,2,1,0:T(8,128)(2,1)} async-done(((bf16[64,4,64,128]{3,2,1,0:T(8,128)(2,1)}), bf16[64,4,64,128]{3,2,1,0:T(8,128)(2,1)}, u32[]{:S(2)}, u32[]{:S(2)}) %all-to-all-start) | async-done | bytes 4194336 | tf_op jit(solution)/shard_map/all_to_all | solution.py:355
  80.0 3.1 %shard_map.72 = (bf16[16,2,64,128]{3,2,1,0:T(8,128)(2,1)}, bf16[16,2,64,128]{3,2,1,0:T(8,128)(2,1)}, bf16[16,2,64,128]{3,2,1,0:T(8,128)(2,1)}, bf16[16,2,64,128]{3,2,1,0:T(8,128)(2,1)}) custom-call(s32[64]{0:T(128)} %copy-done.2, s32[64]{0:T(128)} %broadcast_select_fusion.1.pick_ref, bf16[64,4,64,128]{3,2,1,0:T(8,128)(2,1)} %all-to-all-done.received_ref.slots_ref, ...), custom_call_target="tpu_custom_call" | custom-call | bytes 4194304 | tf_op jit(solution)/shard_map/pallas_call | solution.py:223
  83.2 3.1 %collective-permute-start.2 = (bf16[16,2,64,128]{3,2,1,0:T(8,128)(2,1)}, bf16[16,2,64,128]{3,2,1,0:T(8,128)(2,1)}, u32[]{:S(2)}, u32[]{:S(2)}) collective-permute-start(bf16[16,2,64,128]{3,2,1,0:T(8,128)(2,1)} %get-tuple-element.26), channel_id=1, source_target_pairs={{0,96},{32,0},{64,32},{96,64},{1,97},{33,1},{65,33},{97,65},{2,98}... | collective-permute-start | bytes 1572872 | tf_op jit(solution)/shard_map/ppermute | solution.py:319
  86.4 1.3 collective-permute-done.5.refs_4_
  88.4 4.8 %shard_map.75.refs_6_ = f32[4,512,128]{2,1,0:T(8,128)} custom-call(f32[4]{0:T(128)} %refs_0_.5, s32[2]{0:T(128)} %pad_add_fusion.refs_1_, bf16[22,2,64,128]{3,2,1,0:T(8,128)(2,1)} %get-tuple-element.23.refs_1_.refs_2_, bf16[22,2,64,128]{3,2,1,0:T(8,128)(2,1)} %collective-permute-done.4.refs_3_, bf16[22,2,64,128]{3,2,1,0:T(8,128)(2,1)} %collective-permute-done.5.refs_4_, ...), custom_call_target="tpu_custom_call" | custom-call | flops 590558003200 | bytes 1677721600 | tf_op jit(solution)/shard_map/pallas_call | solution.py:306
  93.2 6.0 %collective-permute-done.1.refs_3_ = bf16[16,2,64,128]{3,2,1,0:T(8,128)(2,1)} collective-permute-done((bf16[16,2,64,128]{3,2,1,0:T(8,128)(2,1)}, bf16[16,2,64,128]{3,2,1,0:T(8,128)(2,1)}, u32[]{:S(2)}, u32[]{:S(2)}) %collective-permute-start.1) | collective-permute-done | bytes 524320 | tf_op jit(solution)/shard_map/ppermute | solution.py:319
  99.2 11.0 %collective-permute-done.2.refs_4_ = bf16[16,2,64,128]{3,2,1,0:T(8,128)(2,1)} collective-permute-done((bf16[16,2,64,128]{3,2,1,0:T(8,128)(2,1)}, bf16[16,2,64,128]{3,2,1,0:T(8,128)(2,1)}, u32[]{:S(2)}, u32[]{:S(2)}) %collective-permute-start.2) | collective-permute-done | bytes 524320 | tf_op jit(solution)/shard_map/ppermute | solution.py:319
  110.2 1.1 collective-permute-done.3.refs_5_
  111.3 4.6 %shard_map.76 = (f32[1024,128]{1,0:T(8,128)}, f32[1024,128]{1,0:T(8,128)}) custom-call(f32[4]{0:T(128)} %refs_0_.5, s32[2]{0:T(128)} %pad_add_fusion.refs_1_, bf16[16,2,64,128]{3,2,1,0:T(8,128)(2,1)} %get-tuple-element.24.refs_2_, bf16[16,2,64,128]{3,2,1,0:T(8,128)(2,1)} %collective-permute-done.1.refs_3_, ...), custom_call_target="tpu_custom_call" | custom-call | flops 1073741824 | bytes 4194304 | tf_op jit(solution)/shard_map/pallas_call | solution.py:306
  116.7 1.7 %collective-permute-done.9 = f32[1024,128]{1,0:T(8,128)S(1)} collective-permute-done((f32[1024,128]{1,0:T(8,128)}, f32[1024,128]{1,0:T(8,128)S(1)}, u32[]{:S(2)}, u32[]{:S(2)}) %collective-permute-start.9) | collective-permute-done | bytes 524320 | tf_op jit(solution)/shard_map/ppermute | solution.py:367
  118.5 1.9 %add.100 = f32[1024,128]{1,0:T(8,128)} add(f32[1024,128]{1,0:T(8,128)} %get-tuple-element.34, f32[1024,128]{1,0:T(8,128)S(1)} %collective-permute-done.9) | non-fusion elementwise | flops 131072 | bytes 1572864 | tf_op jit(solution)/shard_map/add | solution.py:367
  120.4 8.7 %all-to-all-start.1 = ((f32[64,16,128]{2,1,0:T(8,128)}), f32[64,16,128]{2,1,0:T(8,128)S(1)}, u32[]{:S(2)}, u32[]{:S(2)}) async-start(f32[64,16,128]{2,1,0:T(8,128)} %bitcast.4), calls=%async_computation.1 | async-start | bytes 1048576 | tf_op jit(solution)/shard_map/all_to_all | solution.py:368
  129.1 3.3 %shard_map.77 = bf16[4,64,64,128]{3,2,1,0:T(8,128)(2,1)} custom-call(bf16[64,4,64,128]{3,2,1,0:T(8,128)(2,1)} %all-to-all-done.received_ref.slots_ref), custom_call_target="tpu_custom_call" | custom-call | bytes 8388608 | tf_op jit(solution)/shard_map/pallas_call | solution.py:247
  132.4 8.9 %all-to-all-done.1 = f32[64,16,128]{2,1,0:T(8,128)S(1)} async-done(((f32[64,16,128]{2,1,0:T(8,128)}), f32[64,16,128]{2,1,0:T(8,128)S(1)}, u32[]{:S(2)}, u32[]{:S(2)}) %all-to-all-start.1) | async-done | bytes 524320 | tf_op jit(solution)/shard_map/all_to_all | solution.py:368
  (45 shorter events, 11.4 us)
Async XLA Ops:
  0.7 41.7 %copy-start.2 = (s32[64]{0:T(128)}, s32[64]{0:T(128)S(1)}, u32[]{:S(2)}) copy-start(s32[64]{0:T(128)S(1)} %get-tuple-element.38.order_ref) | copy-start | bytes 772
  2.3 7.7 %copy-start = (s32[768]{0:T(1024)S(1)}, s32[768]{0:T(1024)}, u32[]{:S(2)}) copy-start(s32[768]{0:T(1024)} %param.7) | copy-start | bytes 9220
  5.5 37.6 %collective-permute-start = (bf16[16,4,64,128]{3,2,1,0:T(8,128)(2,1)}, bf16[16,4,64,128]{3,2,1,0:T(8,128)(2,1)S(1)}, u32[]{:S(2)}, u32[]{:S(2)}) collective-permute-start(bf16[16,4,64,128]{3,2,1,0:T(8,128)(2,1)} %shard_map.68.refs_4_), channel_id=1, source_target_pairs={{0,64},{32,96},{64,0},{96,32},{1,65},{33,97},{65,1},{97,33},{2,66}... | collective-permute-start | bytes 3145736 | tf_op jit(solution)/shard_map/ppermute | solution.py:319
  10.4 0.7 copy-start.1
  19.7 60.3 %all-to-all-start = ((bf16[64,4,64,128]{3,2,1,0:T(8,128)(2,1)}), bf16[64,4,64,128]{3,2,1,0:T(8,128)(2,1)}, u32[]{:S(2)}, u32[]{:S(2)}) async-start(bf16[64,4,64,128]{3,2,1,0:T(8,128)(2,1)} %get-tuple-element.21), calls=%async_computation | async-start | bytes 8388608 | tf_op jit(solution)/shard_map/all_to_all | solution.py:355
  31.1 25.6 %collective-permute-start.7 = (bf16[16,4,64,128]{3,2,1,0:T(8,128)(2,1)}, bf16[16,4,64,128]{3,2,1,0:T(8,128)(2,1)}, u32[]{:S(2)}, u32[]{:S(2)}) collective-permute-start(bf16[16,4,64,128]{3,2,1,0:T(8,128)(2,1)} %get-tuple-element.32), channel_id=1, source_target_pairs={{0,96},{32,0},{64,32},{96,64},{1,97},{33,1},{65,33},{97,65},{2,98}... | collective-permute-start | bytes 3145736 | tf_op jit(solution)/shard_map/ppermute | solution.py:319
  31.6 25.9 %collective-permute-start.8 = (bf16[16,4,64,128]{3,2,1,0:T(8,128)(2,1)}, bf16[16,4,64,128]{3,2,1,0:T(8,128)(2,1)}, u32[]{:S(2)}, u32[]{:S(2)}) collective-permute-start(bf16[16,4,64,128]{3,2,1,0:T(8,128)(2,1)} %get-tuple-element.33), channel_id=1, source_target_pairs={{0,32},{32,64},{64,96},{96,0},{1,33},{33,65},{65,97},{97,1},{2,34}... | collective-permute-start | bytes 3145736 | tf_op jit(solution)/shard_map/ppermute | solution.py:319
  38.6 47.8 %collective-permute-start.4 = (bf16[22,2,64,128]{3,2,1,0:T(8,128)(2,1)}, bf16[22,2,64,128]{3,2,1,0:T(8,128)(2,1)}, u32[]{:S(2)}, u32[]{:S(2)}) collective-permute-start(bf16[22,2,64,128]{3,2,1,0:T(8,128)(2,1)} %get-tuple-element.28), channel_id=1, source_target_pairs={{0,64},{32,96},{64,0},{96,32},{1,65},{33,97},{65,1},{97,33},{2,66}... | collective-permute-start | bytes 2162696 | tf_op jit(solution)/shard_map/ppermute | solution.py:319
  39.6 48.1 %collective-permute-start.5 = (bf16[22,2,64,128]{3,2,1,0:T(8,128)(2,1)}, bf16[22,2,64,128]{3,2,1,0:T(8,128)(2,1)}, u32[]{:S(2)}, u32[]{:S(2)}) collective-permute-start(bf16[22,2,64,128]{3,2,1,0:T(8,128)(2,1)} %get-tuple-element.29), channel_id=1, source_target_pairs={{0,96},{32,0},{64,32},{96,64},{1,97},{33,1},{65,33},{97,65},{2,98}... | collective-permute-start | bytes 2162696 | tf_op jit(solution)/shard_map/ppermute | solution.py:319
  43.1 1.0 copy-start.3
  43.1 45.3 %collective-permute-start.6 = (bf16[22,2,64,128]{3,2,1,0:T(8,128)(2,1)}, bf16[22,2,64,128]{3,2,1,0:T(8,128)(2,1)}, u32[]{:S(2)}, u32[]{:S(2)}) collective-permute-start(bf16[22,2,64,128]{3,2,1,0:T(8,128)(2,1)} %get-tuple-element.30), channel_id=1, source_target_pairs={{0,32},{32,64},{64,96},{96,0},{1,33},{33,65},{65,97},{97,1},{2,34}... | collective-permute-start | bytes 2162696 | tf_op jit(solution)/shard_map/ppermute | solution.py:319
  83.1 16.1 %collective-permute-start.1 = (bf16[16,2,64,128]{3,2,1,0:T(8,128)(2,1)}, bf16[16,2,64,128]{3,2,1,0:T(8,128)(2,1)}, u32[]{:S(2)}, u32[]{:S(2)}) collective-permute-start(bf16[16,2,64,128]{3,2,1,0:T(8,128)(2,1)} %get-tuple-element.25), channel_id=1, source_target_pairs={{0,64},{32,96},{64,0},{96,32},{1,65},{33,97},{65,1},{97,33},{2,66}... | collective-permute-start | bytes 1572872 | tf_op jit(solution)/shard_map/ppermute | solution.py:319
  83.2 27.0 %collective-permute-start.2 = (bf16[16,2,64,128]{3,2,1,0:T(8,128)(2,1)}, bf16[16,2,64,128]{3,2,1,0:T(8,128)(2,1)}, u32[]{:S(2)}, u32[]{:S(2)}) collective-permute-start(bf16[16,2,64,128]{3,2,1,0:T(8,128)(2,1)} %get-tuple-element.26), channel_id=1, source_target_pairs={{0,96},{32,0},{64,32},{96,64},{1,97},{33,1},{65,33},{97,65},{2,98}... | collective-permute-start | bytes 1572872 | tf_op jit(solution)/shard_map/ppermute | solution.py:319
  86.4 25.0 %collective-permute-start.3 = (bf16[16,2,64,128]{3,2,1,0:T(8,128)(2,1)}, bf16[16,2,64,128]{3,2,1,0:T(8,128)(2,1)}, u32[]{:S(2)}, u32[]{:S(2)}) collective-permute-start(bf16[16,2,64,128]{3,2,1,0:T(8,128)(2,1)} %get-tuple-element.27), channel_id=1, source_target_pairs={{0,32},{32,64},{64,96},{96,0},{1,33},{33,65},{65,97},{97,1},{2,34}... | collective-permute-start | bytes 1572872 | tf_op jit(solution)/shard_map/ppermute | solution.py:319
  115.9 2.5 %collective-permute-start.9 = (f32[1024,128]{1,0:T(8,128)}, f32[1024,128]{1,0:T(8,128)S(1)}, u32[]{:S(2)}, u32[]{:S(2)}) collective-permute-start(f32[1024,128]{1,0:T(8,128)} %get-tuple-element.35), channel_id=1, source_target_pairs={{0,1},{1,0},{2,3},{3,2},{4,5},{5,4},{6,7},{7,6},{8,9},{9,8},{10,11... | collective-permute-start | bytes 1572872 | tf_op jit(solution)/shard_map/ppermute | solution.py:367
  120.4 21.0 %all-to-all-start.1 = ((f32[64,16,128]{2,1,0:T(8,128)}), f32[64,16,128]{2,1,0:T(8,128)S(1)}, u32[]{:S(2)}, u32[]{:S(2)}) async-start(f32[64,16,128]{2,1,0:T(8,128)} %bitcast.4), calls=%async_computation.1 | async-start | bytes 1048576 | tf_op jit(solution)/shard_map/all_to_all | solution.py:368

commit v4 on v3

--- a/solution.py
+++ b/solution.py
@@ -23,6 +23,7 @@
 SMEM = pl.BlockSpec(memory_space=pltpu.SMEM)
 VMEM = pl.BlockSpec(memory_space=pltpu.VMEM)
 PARAMS = pltpu.CompilerParams(vmem_limit_bytes=58 * 2**20)
+SMALL = pltpu.CompilerParams(vmem_limit_bytes=24 * 2**20)
 
 
 def cost(bytes_accessed, flops=0):
@@ -250,7 +251,7 @@
         in_specs=[ANY],
         out_specs=ANY,
         scratch_shapes=[pltpu.VMEM((F, SLOTS, PB, LANES), BF16)] + [pltpu.SemaphoreType.DMA((F,))] * 2,
-        compiler_params=PARAMS,
+        compiler_params=SMALL,
         cost_estimate=cost(8 * 2**20),
     )(slots)
 
@@ -310,7 +311,7 @@
         in_specs=[SMEM, SMEM] + [block] * NZ + [spec for _, spec in more],
         out_specs=[pl.BlockSpec((S * NZ // 2, LANES), lambda f: (0, 0))] * 2 if last else whole,
         scratch_shapes=[pltpu.VMEM((NZ, S, LANES), F32)] if last else [],
-        compiler_params=PARAMS,
+        compiler_params=SMALL,
         cost_estimate=cost(effort * (fields * 2**20 + 2**21), effort * 2 * fields * boxes * PB * S * S),
     )(weight, place, *xs, *[x for x, _ in more])
 

time: 143 us -> 141 us (0.986)
  Pallas kernels: 42 us -> 38.2 us
  other arithmetic: 7.57 us -> 6.11 us
    pallas_call x3, Pallas kernels: 15.3 us -> 11.3 us  [gram(): pl.pallas_call(lambda *refs: gram_kernel(offset, before is not None, scal...]
    ppermute x9, waiting for transfers between devices: 33.1 us -> 34.6 us  [shift(): return lax.ppermute(x, 'snap', [(i, (i + by) % NZ) for i in range(NZ)])]
  transfers between devices with their start and end apart: 12 -> 12, of which waited for: 10 -> 10; matrix products, arithmetic and copies ran while one was open for 3% -> 2% of each run, Pallas kernels for 24% -> 23%
where the time goes in v4:
time: 141 us; the launch traced here: 139 us
  waiting for transfers between devices  61.7 us (44%)
  Pallas kernels  38.2 us (27%)
  starting transfers between devices  30.1 us (21%)
  other arithmetic  6.11 us (4%)
  local copies, waits for them, and re-layouts  2.5 us (2%)
    ppermute x9, waiting for transfers between devices, shift(): return lax.ppermute(x, 'snap', [(i, (i + by) % NZ) for i in range(NZ)])  34.6 us
    all_to_all x1, waiting for transfers between devices, on_device(): lax.all_to_all(outgoing, XY, split_axis=0, concat_axis=0, tiled=True)  16.6 us
    ppermute x9, starting transfers between devices, shift(): return lax.ppermute(x, 'snap', [(i, (i + by) % NZ) for i in range(NZ)])  12.5 us
    pallas_call x3, Pallas kernels, gram(): pl.pallas_call(lambda *refs: gram_kernel(offset, before is not None, scal...  11.3 us
    all_to_all x1, waiting for transfers between devices, on_device(): lax.all_to_all(shares, ('snap', 'tile'), split_axis=0, concat_axis=0, til...  8.91 us
    pallas_call x1, Pallas kernels, restrict(): pl.pallas_call(lambda *refs: restrict_kernel(steps, group, fields, *refs)...  8.64 us
    all_to_all x1, starting transfers between devices, on_device(): lax.all_to_all(shares, ('snap', 'tile'), split_axis=0, concat_axis=0, til...  8.64 us
    all_to_all x1, starting transfers between devices, on_device(): lax.all_to_all(outgoing, XY, split_axis=0, concat_axis=0, tiled=True)  8.1 us
  transfers between devices with their start and end apart: 12, of which 10 were waited for; matrix products, arithmetic and copies ran while one was open for 2% of the time, Pallas kernels for 23%

profile of v4, /device:TPU:1, one launch (start us, length us, event | category | flops | bytes accessed | tf_op | source)
XLA Modules:
  0.0 139.4 jit_solution(12617625375453060626)
XLA Ops:
  2.4 3.1 %shard_map.68.refs_4_ = bf16[16,4,64,128]{3,2,1,0:T(8,128)(2,1)} custom-call(s32[64]{0:T(128)} %select_reduce_fusion.2.refs_0_.first_ref, bf16[4,128,64,128]{3,2,1,0:T(8,128)(2,1)} %bitcast.10, f32[4]{0:T(128)} %refs_0_.5), custom_call_target="tpu_custom_call" | custom-call | bytes 2097152 | tf_op jit(solution)/shard_map/pallas_call | solution.py:83
  5.5 4.5 %collective-permute-start = (bf16[16,4,64,128]{3,2,1,0:T(8,128)(2,1)}, bf16[16,4,64,128]{3,2,1,0:T(8,128)(2,1)S(1)}, u32[]{:S(2)}, u32[]{:S(2)}) collective-permute-start(bf16[16,4,64,128]{3,2,1,0:T(8,128)(2,1)} %shard_map.68.refs_4_), channel_id=1, source_target_pairs={{0,64},{32,96},{64,0},{96,32},{1,65},{33,97},{65,1},{97,33},{2,66}... | collective-permute-start | bytes 3145736 | tf_op jit(solution)/shard_map/ppermute | solution.py:320
  11.0 8.6 %shard_map.69 = (bf16[64,4,64,128]{3,2,1,0:T(8,128)(2,1)}, bf16[24,2,64,128]{3,2,1,0:T(8,128)(2,1)}) custom-call(s32[24]{0:T(128)} %copy-done.7, s32[64]{0:T(128)} %convert_element_type.23.refs_1_, s32[1,512]{1,0:T(1,128)} %bitcast.15, bf16[24,4,512,128]{3,2,1,0:T(8,128)(2,1)} %refs_3_.1, bf16[16,4,64,128]{3,2,1,0:T(8,128)(2,1)} %shard_map.68.refs_4_), custom_call_target="tpu_custom_call" | custom-call | flops 805306368 | bytes 16777216 | tf_op jit(solution)/shard_map/pallas_call | solution.py:129
  19.7 8.1 %all-to-all-start = ((bf16[64,4,64,128]{3,2,1,0:T(8,128)(2,1)}), bf16[64,4,64,128]{3,2,1,0:T(8,128)(2,1)}, u32[]{:S(2)}, u32[]{:S(2)}) async-start(bf16[64,4,64,128]{3,2,1,0:T(8,128)(2,1)} %get-tuple-element.21), calls=%async_computation | async-start | bytes 8388608 | tf_op jit(solution)/shard_map/all_to_all | solution.py:356
  27.8 3.4 %shard_map.73 = (bf16[16,4,64,128]{3,2,1,0:T(8,128)(2,1)}, bf16[16,4,64,128]{3,2,1,0:T(8,128)(2,1)}) custom-call(s32[64]{0:T(128)} %select_reduce_fusion.2.refs_0_.first_ref, bf16[4,128,64,128]{3,2,1,0:T(8,128)(2,1)} %bitcast.11, bf16[24,2,64,128]{3,2,1,0:T(8,128)(2,1)} %get-tuple-element.22.patches_ref.refs_2_), custom_call_target="tpu_custom_call" | custom-call | bytes 4194304 | tf_op jit(solution)/shard_map/pallas_call | solution.py:83
  34.1 4.9 %shard_map.70 = (bf16[22,2,64,128]{3,2,1,0:T(8,128)(2,1)}, bf16[22,2,64,128]{3,2,1,0:T(8,128)(2,1)}, bf16[22,2,64,128]{3,2,1,0:T(8,128)(2,1)}, bf16[22,2,64,128]{3,2,1,0:T(8,128)(2,1)}, bf16[16,4,64,128]{3,2,1,0:T(8,128)(2,1)}) custom-call(s32[1]{0:T(128)} %bitcast.z_ref, s32[64]{0:T(128)} %broadcast_add_fusion.2.late_ref, ...), custom_call_target="tpu_custom_call" | custom-call | bytes 4194304 | tf_op jit(solution)/shard_map/pallas_call | solution.py:186
  39.0 1.1 collective-permute-start.4
  40.0 2.1 %collective-permute-start.5 = (bf16[22,2,64,128]{3,2,1,0:T(8,128)(2,1)}, bf16[22,2,64,128]{3,2,1,0:T(8,128)(2,1)}, u32[]{:S(2)}, u32[]{:S(2)}) collective-permute-start(bf16[22,2,64,128]{3,2,1,0:T(8,128)(2,1)} %get-tuple-element.29), channel_id=1, source_target_pairs={{0,96},{32,0},{64,32},{96,64},{1,97},{33,1},{65,33},{97,65},{2,98}... | collective-permute-start | bytes 2162696 | tf_op jit(solution)/shard_map/ppermute | solution.py:320
  44.5 12.3 %collective-permute-done.7.refs_4_ = bf16[16,4,64,128]{3,2,1,0:T(8,128)(2,1)} collective-permute-done((bf16[16,4,64,128]{3,2,1,0:T(8,128)(2,1)}, bf16[16,4,64,128]{3,2,1,0:T(8,128)(2,1)}, u32[]{:S(2)}, u32[]{:S(2)}) %collective-permute-start.7) | collective-permute-done | bytes 1048608 | tf_op jit(solution)/shard_map/ppermute | solution.py:320
  57.6 1.2 copy-done.2
  58.8 4.6 %shard_map.74.refs_6_ = f32[4,512,128]{2,1,0:T(8,128)S(1)} custom-call(f32[4]{0:T(128)S(1)} %copy-done, s32[2]{0:T(128)S(1)} %pad_add_fusion.refs_1_, bf16[16,4,64,128]{3,2,1,0:T(8,128)(2,1)S(1)} %copy-done.3, bf16[16,4,64,128]{3,2,1,0:T(8,128)(2,1)S(1)} %copy-done.2, bf16[16,4,64,128]{3,2,1,0:T(8,128)(2,1)} %collective-permute-done.7.refs_4_, ...), custom_call_target="tpu_custom_call" | custom-call | flops 858993459200 | bytes 2516582400 | tf_op jit(solution)/shard_map/pallas_call | solution.py:307
  63.4 16.6 %all-to-all-done.received_ref.slots_ref = bf16[64,4,64,128]{3,2,1,0:T(8,128)(2,1)} async-done(((bf16[64,4,64,128]{3,2,1,0:T(8,128)(2,1)}), bf16[64,4,64,128]{3,2,1,0:T(8,128)(2,1)}, u32[]{:S(2)}, u32[]{:S(2)}) %all-to-all-start) | async-done | bytes 4194336 | tf_op jit(solution)/shard_map/all_to_all | solution.py:356
  80.0 3.1 %shard_map.72 = (bf16[16,2,64,128]{3,2,1,0:T(8,128)(2,1)}, bf16[16,2,64,128]{3,2,1,0:T(8,128)(2,1)}, bf16[16,2,64,128]{3,2,1,0:T(8,128)(2,1)}, bf16[16,2,64,128]{3,2,1,0:T(8,128)(2,1)}) custom-call(s32[64]{0:T(128)} %copy-done.8, s32[64]{0:T(128)} %broadcast_select_fusion.1.pick_ref, bf16[64,4,64,128]{3,2,1,0:T(8,128)(2,1)} %all-to-all-done.received_ref.slots_ref, ...), custom_call_target="tpu_custom_call" | custom-call | bytes 4194304 | tf_op jit(solution)/shard_map/pallas_call | solution.py:224
  83.2 3.1 %collective-permute-start.2 = (bf16[16,2,64,128]{3,2,1,0:T(8,128)(2,1)}, bf16[16,2,64,128]{3,2,1,0:T(8,128)(2,1)}, u32[]{:S(2)}, u32[]{:S(2)}) collective-permute-start(bf16[16,2,64,128]{3,2,1,0:T(8,128)(2,1)} %get-tuple-element.26), channel_id=1, source_target_pairs={{0,96},{32,0},{64,32},{96,64},{1,97},{33,1},{65,33},{97,65},{2,98}... | collective-permute-start | bytes 1572872 | tf_op jit(solution)/shard_map/ppermute | solution.py:320
  86.3 1.4 %collective-permute-done.5.refs_4_ = bf16[22,2,64,128]{3,2,1,0:T(8,128)(2,1)} collective-permute-done((bf16[22,2,64,128]{3,2,1,0:T(8,128)(2,1)}, bf16[22,2,64,128]{3,2,1,0:T(8,128)(2,1)}, u32[]{:S(2)}, u32[]{:S(2)}) %collective-permute-start.5) | collective-permute-done | bytes 720928 | tf_op jit(solution)/shard_map/ppermute | solution.py:320
  88.4 3.5 %shard_map.75.refs_6_ = f32[4,512,128]{2,1,0:T(8,128)S(1)} custom-call(f32[4]{0:T(128)S(1)} %copy-done, s32[2]{0:T(128)S(1)} %pad_add_fusion.refs_1_, bf16[22,2,64,128]{3,2,1,0:T(8,128)(2,1)S(1)} %copy-done.4, bf16[22,2,64,128]{3,2,1,0:T(8,128)(2,1)} %collective-permute-done.4.refs_3_, bf16[22,2,64,128]{3,2,1,0:T(8,128)(2,1)} %collective-permute-done.5.refs_4_, ...), custom_call_target="tpu_custom_call" | custom-call | flops 590558003200 | bytes 1677721600 | tf_op jit(solution)/shard_map/pallas_call | solution.py:307
  91.9 7.4 %collective-permute-done.1.refs_3_ = bf16[16,2,64,128]{3,2,1,0:T(8,128)(2,1)} collective-permute-done((bf16[16,2,64,128]{3,2,1,0:T(8,128)(2,1)}, bf16[16,2,64,128]{3,2,1,0:T(8,128)(2,1)}, u32[]{:S(2)}, u32[]{:S(2)}) %collective-permute-start.1) | collective-permute-done | bytes 524320 | tf_op jit(solution)/shard_map/ppermute | solution.py:320
  99.3 11.0 %collective-permute-done.2.refs_4_ = bf16[16,2,64,128]{3,2,1,0:T(8,128)(2,1)} collective-permute-done((bf16[16,2,64,128]{3,2,1,0:T(8,128)(2,1)}, bf16[16,2,64,128]{3,2,1,0:T(8,128)(2,1)}, u32[]{:S(2)}, u32[]{:S(2)}) %collective-permute-start.2) | collective-permute-done | bytes 524320 | tf_op jit(solution)/shard_map/ppermute | solution.py:320
  110.3 1.1 collective-permute-done.3.refs_5_
  111.4 3.2 %shard_map.76 = (f32[1024,128]{1,0:T(8,128)S(1)}, f32[1024,128]{1,0:T(8,128)S(1)}) custom-call(f32[4]{0:T(128)S(1)} %copy-done, s32[2]{0:T(128)S(1)} %pad_add_fusion.refs_1_, bf16[16,2,64,128]{3,2,1,0:T(8,128)(2,1)S(1)} %copy-done.5, bf16[16,2,64,128]{3,2,1,0:T(8,128)(2,1)} %collective-permute-done.1.refs_3_, ...), custom_call_target="tpu_custom_call" | custom-call | flops 1073741824 | bytes 4194304 | tf_op jit(solution)/shard_map/pallas_call | solution.py:307
  115.5 1.5 %collective-permute-done.9 = f32[1024,128]{1,0:T(8,128)S(1)} collective-permute-done((f32[1024,128]{1,0:T(8,128)S(1)}, f32[1024,128]{1,0:T(8,128)S(1)}, u32[]{:S(2)}, u32[]{:S(2)}) %collective-permute-start.9) | collective-permute-done | bytes 524320 | tf_op jit(solution)/shard_map/ppermute | solution.py:368
  117.8 8.6 %all-to-all-start.1 = ((f32[64,16,128]{2,1,0:T(8,128)}), f32[64,16,128]{2,1,0:T(8,128)S(1)}, u32[]{:S(2)}, u32[]{:S(2)}) async-start(f32[64,16,128]{2,1,0:T(8,128)} %bitcast.4), calls=%async_computation.1 | async-start | bytes 1048576 | tf_op jit(solution)/shard_map/all_to_all | solution.py:369
  126.5 3.3 %shard_map.77 = bf16[4,64,64,128]{3,2,1,0:T(8,128)(2,1)} custom-call(bf16[64,4,64,128]{3,2,1,0:T(8,128)(2,1)} %all-to-all-done.received_ref.slots_ref), custom_call_target="tpu_custom_call" | custom-call | bytes 8388608 | tf_op jit(solution)/shard_map/pallas_call | solution.py:248
  129.8 8.9 %all-to-all-done.1 = f32[64,16,128]{2,1,0:T(8,128)S(1)} async-done(((f32[64,16,128]{2,1,0:T(8,128)}), f32[64,16,128]{2,1,0:T(8,128)S(1)}, u32[]{:S(2)}, u32[]{:S(2)}) %all-to-all-start.1) | async-done | bytes 524320 | tf_op jit(solution)/shard_map/all_to_all | solution.py:369
  (55 shorter events, 11.9 us)
Async XLA Ops:
  0.7 41.6 %copy-start.8 = (s32[64]{0:T(128)}, s32[64]{0:T(128)S(1)}, u32[]{:S(2)}) copy-start(s32[64]{0:T(128)S(1)} %get-tuple-element.38.order_ref) | copy-start | bytes 772
  2.4 7.6 %copy-start.6 = (s32[768]{0:T(1024)S(1)}, s32[768]{0:T(1024)}, u32[]{:S(2)}) copy-start(s32[768]{0:T(1024)} %param.7) | copy-start | bytes 9220
  5.5 37.5 %collective-permute-start = (bf16[16,4,64,128]{3,2,1,0:T(8,128)(2,1)}, bf16[16,4,64,128]{3,2,1,0:T(8,128)(2,1)S(1)}, u32[]{:S(2)}, u32[]{:S(2)}) collective-permute-start(bf16[16,4,64,128]{3,2,1,0:T(8,128)(2,1)} %shard_map.68.refs_4_), channel_id=1, source_target_pairs={{0,64},{32,96},{64,0},{96,32},{1,65},{33,97},{65,1},{97,33},{2,66}... | collective-permute-start | bytes 3145736 | tf_op jit(solution)/shard_map/ppermute | solution.py:320
  10.3 0.7 copy-start.7
  19.7 60.3 %all-to-all-start = ((bf16[64,4,64,128]{3,2,1,0:T(8,128)(2,1)}), bf16[64,4,64,128]{3,2,1,0:T(8,128)(2,1)}, u32[]{:S(2)}, u32[]{:S(2)}) async-start(bf16[64,4,64,128]{3,2,1,0:T(8,128)(2,1)} %get-tuple-element.21), calls=%async_computation | async-start | bytes 8388608 | tf_op jit(solution)/shard_map/all_to_all | solution.py:356
  31.2 25.6 %collective-permute-start.7 = (bf16[16,4,64,128]{3,2,1,0:T(8,128)(2,1)}, bf16[16,4,64,128]{3,2,1,0:T(8,128)(2,1)}, u32[]{:S(2)}, u32[]{:S(2)}) collective-permute-start(bf16[16,4,64,128]{3,2,1,0:T(8,128)(2,1)} %get-tuple-element.32), channel_id=1, source_target_pairs={{0,96},{32,0},{64,32},{96,64},{1,97},{33,1},{65,33},{97,65},{2,98}... | collective-permute-start | bytes 3145736 | tf_op jit(solution)/shard_map/ppermute | solution.py:320
  31.7 25.9 %collective-permute-start.8 = (bf16[16,4,64,128]{3,2,1,0:T(8,128)(2,1)}, bf16[16,4,64,128]{3,2,1,0:T(8,128)(2,1)}, u32[]{:S(2)}, u32[]{:S(2)}) collective-permute-start(bf16[16,4,64,128]{3,2,1,0:T(8,128)(2,1)} %get-tuple-element.33), channel_id=1, source_target_pairs={{0,32},{32,64},{64,96},{96,0},{1,33},{33,65},{65,97},{97,1},{2,34}... | collective-permute-start | bytes 3145736 | tf_op jit(solution)/shard_map/ppermute | solution.py:320
  39.0 47.3 %collective-permute-start.4 = (bf16[22,2,64,128]{3,2,1,0:T(8,128)(2,1)}, bf16[22,2,64,128]{3,2,1,0:T(8,128)(2,1)}, u32[]{:S(2)}, u32[]{:S(2)}) collective-permute-start(bf16[22,2,64,128]{3,2,1,0:T(8,128)(2,1)} %get-tuple-element.28), channel_id=1, source_target_pairs={{0,64},{32,96},{64,0},{96,32},{1,65},{33,97},{65,1},{97,33},{2,66}... | collective-permute-start | bytes 2162696 | tf_op jit(solution)/shard_map/ppermute | solution.py:320
  40.0 47.7 %collective-permute-start.5 = (bf16[22,2,64,128]{3,2,1,0:T(8,128)(2,1)}, bf16[22,2,64,128]{3,2,1,0:T(8,128)(2,1)}, u32[]{:S(2)}, u32[]{:S(2)}) collective-permute-start(bf16[22,2,64,128]{3,2,1,0:T(8,128)(2,1)} %get-tuple-element.29), channel_id=1, source_target_pairs={{0,96},{32,0},{64,32},{96,64},{1,97},{33,1},{65,33},{97,65},{2,98}... | collective-permute-start | bytes 2162696 | tf_op jit(solution)/shard_map/ppermute | solution.py:320
  43.0 1.0 copy-start.1
  43.0 45.5 %collective-permute-start.6 = (bf16[22,2,64,128]{3,2,1,0:T(8,128)(2,1)}, bf16[22,2,64,128]{3,2,1,0:T(8,128)(2,1)}, u32[]{:S(2)}, u32[]{:S(2)}) collective-permute-start(bf16[22,2,64,128]{3,2,1,0:T(8,128)(2,1)} %get-tuple-element.30), channel_id=1, source_target_pairs={{0,32},{32,64},{64,96},{96,0},{1,33},{33,65},{65,97},{97,1},{2,34}... | collective-permute-start | bytes 2162696 | tf_op jit(solution)/shard_map/ppermute | solution.py:320
  43.9 13.6 %copy-start = (f32[4]{0:T(128)S(1)}, f32[4]{0:T(128)}, u32[]{:S(2)}) copy-start(f32[4]{0:T(128)} %refs_0_.5) | copy-start | bytes 52
  43.9 13.6 %copy-start.3 = (bf16[16,4,64,128]{3,2,1,0:T(8,128)(2,1)S(1)}, bf16[16,4,64,128]{3,2,1,0:T(8,128)(2,1)}, u32[]{:S(2)}) copy-start(bf16[16,4,64,128]{3,2,1,0:T(8,128)(2,1)} %get-tuple-element.31.refs_2_) | copy-start | bytes 3145732
  57.6 1.2 copy-start.2
  63.4 25.0 %copy-start.4 = (bf16[22,2,64,128]{3,2,1,0:T(8,128)(2,1)S(1)}, bf16[22,2,64,128]{3,2,1,0:T(8,128)(2,1)}, u32[]{:S(2)}) copy-start(bf16[22,2,64,128]{3,2,1,0:T(8,128)(2,1)} %get-tuple-element.23.refs_1_.refs_2_) | copy-start | bytes 2162692
  83.1 16.2 %collective-permute-start.1 = (bf16[16,2,64,128]{3,2,1,0:T(8,128)(2,1)}, bf16[16,2,64,128]{3,2,1,0:T(8,128)(2,1)}, u32[]{:S(2)}, u32[]{:S(2)}) collective-permute-start(bf16[16,2,64,128]{3,2,1,0:T(8,128)(2,1)} %get-tuple-element.25), channel_id=1, source_target_pairs={{0,64},{32,96},{64,0},{96,32},{1,65},{33,97},{65,1},{97,33},{2,66}... | collective-permute-start | bytes 1572872 | tf_op jit(solution)/shard_map/ppermute | solution.py:320
  83.2 27.1 %collective-permute-start.2 = (bf16[16,2,64,128]{3,2,1,0:T(8,128)(2,1)}, bf16[16,2,64,128]{3,2,1,0:T(8,128)(2,1)}, u32[]{:S(2)}, u32[]{:S(2)}) collective-permute-start(bf16[16,2,64,128]{3,2,1,0:T(8,128)(2,1)} %get-tuple-element.26), channel_id=1, source_target_pairs={{0,96},{32,0},{64,32},{96,64},{1,97},{33,1},{65,33},{97,65},{2,98}... | collective-permute-start | bytes 1572872 | tf_op jit(solution)/shard_map/ppermute | solution.py:320
  86.3 25.1 %collective-permute-start.3 = (bf16[16,2,64,128]{3,2,1,0:T(8,128)(2,1)}, bf16[16,2,64,128]{3,2,1,0:T(8,128)(2,1)}, u32[]{:S(2)}, u32[]{:S(2)}) collective-permute-start(bf16[16,2,64,128]{3,2,1,0:T(8,128)(2,1)} %get-tuple-element.27), channel_id=1, source_target_pairs={{0,32},{32,64},{64,96},{96,0},{1,33},{33,65},{65,97},{97,1},{2,34}... | collective-permute-start | bytes 1572872 | tf_op jit(solution)/shard_map/ppermute | solution.py:320
  88.4 22.9 %copy-start.5 = (bf16[16,2,64,128]{3,2,1,0:T(8,128)(2,1)S(1)}, bf16[16,2,64,128]{3,2,1,0:T(8,128)(2,1)}, u32[]{:S(2)}) copy-start(bf16[16,2,64,128]{3,2,1,0:T(8,128)(2,1)} %get-tuple-element.24.refs_2_) | copy-start | bytes 1572868
  114.6 2.4 %collective-permute-start.9 = (f32[1024,128]{1,0:T(8,128)S(1)}, f32[1024,128]{1,0:T(8,128)S(1)}, u32[]{:S(2)}, u32[]{:S(2)}) collective-permute-start(f32[1024,128]{1,0:T(8,128)S(1)} %get-tuple-element.35), channel_id=1, source_target_pairs={{0,1},{1,0},{2,3},{3,2},{4,5},{5,4},{6,7},{7,6},{8,9},{9,8},{10,11... | collective-permute-start | bytes 1572872 | tf_op jit(solution)/shard_map/ppermute | solution.py:368
  117.8 20.9 %all-to-all-start.1 = ((f32[64,16,128]{2,1,0:T(8,128)}), f32[64,16,128]{2,1,0:T(8,128)S(1)}, u32[]{:S(2)}, u32[]{:S(2)}) async-start(f32[64,16,128]{2,1,0:T(8,128)} %bitcast.4), calls=%async_computation.1 | async-start | bytes 1048576 | tf_op jit(solution)/shard_map/all_to_all | solution.py:369

commit v5 on v4

--- a/solution.py
+++ b/solution.py
@@ -12,6 +12,7 @@
 OWNERS = 32
 LANES = 128
 QUARTER = SLOTS // NZ
+LOT = 4
 EARLY = 2
 S = NZ * LANES
 SEND_ORDER = (2, 1, 3, 0)
@@ -63,9 +64,10 @@
 
 
 def stage_out(stage, outs, into, away):
-    for n, out in enumerate(outs):
-        pltpu.make_async_copy(out, stage.at[n], into.at[n]).wait()
-        pltpu.make_async_copy(stage.at[n], out, away.at[n]).start()
+    lots = [(n, c, out, pl.ds(c * LOT, LOT)) for n, out in enumerate(outs) for c in range(QUARTER // LOT)]
+    for n, c, out, part in lots:
+        pltpu.make_async_copy(out.at[part], stage.at[n, part], into.at[n, c]).wait()
+        pltpu.make_async_copy(stage.at[n, part], out.at[part], away.at[n]).start()
     for n, out in enumerate(outs):
         pltpu.make_async_copy(stage.at[n], out, away.at[n]).wait()
 
@@ -74,7 +76,7 @@
     outs, (stage, into, away) = rest[:-3], rest[-3:]
     for n, r in enumerate(parts):
         for j in range(QUARTER):
-            pltpu.make_async_copy(coarse_ref.at[:, first_ref[r * QUARTER + j]], stage.at[n, j], into.at[n]).start()
+            pltpu.make_async_copy(coarse_ref.at[:, first_ref[r * QUARTER + j]], stage.at[n, j], into.at[n, j // LOT]).start()
     stage_out(stage, outs, into, away)
 
 
@@ -85,7 +87,7 @@
         out_shape=[jax.ShapeDtypeStruct(shape, BF16) for _ in parts],
         in_specs=[SMEM, ANY, ANY],
         out_specs=[ANY for _ in parts],
-        scratch_shapes=[pltpu.VMEM((len(parts), *shape), BF16)] + [pltpu.SemaphoreType.DMA((NZ,))] * 2,
+        scratch_shapes=[pltpu.VMEM((len(parts), *shape), BF16)] + [pltpu.SemaphoreType.DMA((NZ, QUARTER // LOT)), pltpu.SemaphoreType.DMA((NZ,))],
         compiler_params=PARAMS,
         cost_estimate=cost(2 * len(parts) * QUARTER * F * PB * LANES * 2),
     )(first, coarse, after)
@@ -210,11 +212,11 @@
 
             @pl.when(box < 0)
             def _(n=n, j=j, k=k):
-                pltpu.make_async_copy(received_ref.at[order_ref[k], fields], stage.at[n, j], into.at[n]).start()
+                pltpu.make_async_copy(received_ref.at[order_ref[k], fields], stage.at[n, j], into.at[n, j // LOT]).start()
 
             @pl.when(box >= 0)
             def _(n=n, j=j, box=box):
-                pltpu.make_async_copy(coarse_ref.at[fields, box], stage.at[n, j], into.at[n]).start()
+                pltpu.make_async_copy(coarse_ref.at[fields, box], stage.at[n, j], into.at[n, j // LOT]).start()
 
     stage_out(stage, [outs[r] for r in SEND_ORDER], into, away)
 
@@ -226,7 +228,7 @@
         out_shape=[jax.ShapeDtypeStruct(shape, BF16)] * NZ,
         in_specs=[SMEM, SMEM, ANY, ANY, ANY],
         out_specs=[ANY] * NZ,
-        scratch_shapes=[pltpu.VMEM((NZ, *shape), BF16)] + [pltpu.SemaphoreType.DMA((NZ,))] * 2,
+        scratch_shapes=[pltpu.VMEM((NZ, *shape), BF16)] + [pltpu.SemaphoreType.DMA((NZ, QUARTER // LOT)), pltpu.SemaphoreType.DMA((NZ,))],
         compiler_params=PARAMS,
         cost_estimate=cost(4 * 2**20),
     )(order, pick, received, coarse, after)

time: 141 us -> 141 us (level)
  waiting for transfers between devices: 61.7 us -> 58.8 us
  Pallas kernels: 38.2 us -> 41 us
    pallas_call x1, Pallas kernels: 4.87 us -> 7.9 us  [local_part(): pl.pallas_call(local_kernel, out_shape=[jax.ShapeDtypeStruct(shape, BF16)...]
    ppermute x9, waiting for transfers between devices: 34.6 us -> 31.7 us  [shift(): return lax.ppermute(x, 'snap', [(i, (i + by) % NZ) for i in range(NZ)])]
  transfers between devices with their start and end apart: 12 -> 12, of which waited for: 10 -> 10; matrix products, arithmetic and copies ran while one was open for 2% -> 2% of each run, Pallas kernels for 23% -> 25%
where the time goes in v5:
time: 141 us; the launch traced here: 139 us
  waiting for transfers between devices  58.8 us (42%)
  Pallas kernels  41 us (29%)
  starting transfers between devices  30 us (21%)
  other arithmetic  6.11 us (4%)
  local copies, waits for them, and re-layouts  2.5 us (2%)
    ppermute x9, waiting for transfers between devices, shift(): return lax.ppermute(x, 'snap', [(i, (i + by) % NZ) for i in range(NZ)])  31.7 us
    all_to_all x1, waiting for transfers between devices, on_device(): lax.all_to_all(outgoing, XY, split_axis=0, concat_axis=0, tiled=True)  16.7 us
    ppermute x9, starting transfers between devices, shift(): return lax.ppermute(x, 'snap', [(i, (i + by) % NZ) for i in range(NZ)])  12.3 us
    pallas_call x3, Pallas kernels, gram(): pl.pallas_call(lambda *refs: gram_kernel(offset, before is not None, scal...  11.3 us
    all_to_all x1, waiting for transfers between devices, on_device(): lax.all_to_all(shares, ('snap', 'tile'), split_axis=0, concat_axis=0, til...  8.91 us
    all_to_all x1, starting transfers between devices, on_device(): lax.all_to_all(shares, ('snap', 'tile'), split_axis=0, concat_axis=0, til...  8.77 us
    pallas_call x1, Pallas kernels, restrict(): pl.pallas_call(lambda *refs: restrict_kernel(steps, group, fields, *refs)...  8.64 us
    all_to_all x1, starting transfers between devices, on_device(): lax.all_to_all(outgoing, XY, split_axis=0, concat_axis=0, tiled=True)  8.11 us
  transfers between devices with their start and end apart: 12, of which 10 were waited for; matrix products, arithmetic and copies ran while one was open for 2% of the time, Pallas kernels for 25%

profile of v5, /device:TPU:1, one launch (start us, length us, event | category | flops | bytes accessed | tf_op | source)
XLA Modules:
  0.0 139.3 jit_solution(3882295517945776202)
XLA Ops:
  2.4 3.0 %shard_map.68.refs_4_ = bf16[16,4,64,128]{3,2,1,0:T(8,128)(2,1)} custom-call(s32[64]{0:T(128)} %select_reduce_fusion.2.refs_0_.first_ref, bf16[4,128,64,128]{3,2,1,0:T(8,128)(2,1)} %bitcast.10, f32[4]{0:T(128)} %refs_0_.5), custom_call_target="tpu_custom_call" | custom-call | bytes 2097152 | tf_op jit(solution)/shard_map/pallas_call | solution.py:85
  5.3 4.5 %collective-permute-start = (bf16[16,4,64,128]{3,2,1,0:T(8,128)(2,1)}, bf16[16,4,64,128]{3,2,1,0:T(8,128)(2,1)S(1)}, u32[]{:S(2)}, u32[]{:S(2)}) collective-permute-start(bf16[16,4,64,128]{3,2,1,0:T(8,128)(2,1)} %shard_map.68.refs_4_), channel_id=1, source_target_pairs={{0,64},{32,96},{64,0},{96,32},{1,65},{33,97},{65,1},{97,33},{2,66}... | collective-permute-start | bytes 3145736 | tf_op jit(solution)/shard_map/ppermute | solution.py:322
  10.9 8.6 %shard_map.69 = (bf16[64,4,64,128]{3,2,1,0:T(8,128)(2,1)}, bf16[24,2,64,128]{3,2,1,0:T(8,128)(2,1)}) custom-call(s32[24]{0:T(128)} %copy-done.7, s32[64]{0:T(128)} %convert_element_type.23.refs_1_, s32[1,512]{1,0:T(1,128)} %bitcast.15, bf16[24,4,512,128]{3,2,1,0:T(8,128)(2,1)} %refs_3_.1, bf16[16,4,64,128]{3,2,1,0:T(8,128)(2,1)} %shard_map.68.refs_4_), custom_call_target="tpu_custom_call" | custom-call | flops 805306368 | bytes 16777216 | tf_op jit(solution)/shard_map/pallas_call | solution.py:131
  19.5 8.1 %all-to-all-start = ((bf16[64,4,64,128]{3,2,1,0:T(8,128)(2,1)}), bf16[64,4,64,128]{3,2,1,0:T(8,128)(2,1)}, u32[]{:S(2)}, u32[]{:S(2)}) async-start(bf16[64,4,64,128]{3,2,1,0:T(8,128)(2,1)} %get-tuple-element.21), calls=%async_computation | async-start | bytes 8388608 | tf_op jit(solution)/shard_map/all_to_all | solution.py:358
  27.7 3.2 %shard_map.73 = (bf16[16,4,64,128]{3,2,1,0:T(8,128)(2,1)}, bf16[16,4,64,128]{3,2,1,0:T(8,128)(2,1)}) custom-call(s32[64]{0:T(128)} %select_reduce_fusion.2.refs_0_.first_ref, bf16[4,128,64,128]{3,2,1,0:T(8,128)(2,1)} %bitcast.11, bf16[24,2,64,128]{3,2,1,0:T(8,128)(2,1)} %get-tuple-element.22.patches_ref.refs_2_), custom_call_target="tpu_custom_call" | custom-call | bytes 4194304 | tf_op jit(solution)/shard_map/pallas_call | solution.py:85
  33.8 7.9 %shard_map.70 = (bf16[22,2,64,128]{3,2,1,0:T(8,128)(2,1)}, bf16[22,2,64,128]{3,2,1,0:T(8,128)(2,1)}, bf16[22,2,64,128]{3,2,1,0:T(8,128)(2,1)}, bf16[22,2,64,128]{3,2,1,0:T(8,128)(2,1)}, bf16[16,4,64,128]{3,2,1,0:T(8,128)(2,1)}) custom-call(s32[1]{0:T(128)} %bitcast.z_ref, s32[64]{0:T(128)} %broadcast_add_fusion.2.late_ref, ...), custom_call_target="tpu_custom_call" | custom-call | bytes 4194304 | tf_op jit(solution)/shard_map/pallas_call | solution.py:188
  41.7 1.1 collective-permute-start.4
  42.8 2.0 %collective-permute-start.5 = (bf16[22,2,64,128]{3,2,1,0:T(8,128)(2,1)}, bf16[22,2,64,128]{3,2,1,0:T(8,128)(2,1)}, u32[]{:S(2)}, u32[]{:S(2)}) collective-permute-start(bf16[22,2,64,128]{3,2,1,0:T(8,128)(2,1)} %get-tuple-element.29), channel_id=1, source_target_pairs={{0,96},{32,0},{64,32},{96,64},{1,97},{33,1},{65,33},{97,65},{2,98}... | collective-permute-start | bytes 2162696 | tf_op jit(solution)/shard_map/ppermute | solution.py:322
  47.2 9.4 %collective-permute-done.7.refs_4_ = bf16[16,4,64,128]{3,2,1,0:T(8,128)(2,1)} collective-permute-done((bf16[16,4,64,128]{3,2,1,0:T(8,128)(2,1)}, bf16[16,4,64,128]{3,2,1,0:T(8,128)(2,1)}, u32[]{:S(2)}, u32[]{:S(2)}) %collective-permute-start.7) | collective-permute-done | bytes 1048608 | tf_op jit(solution)/shard_map/ppermute | solution.py:322
  57.3 1.2 copy-done.2
  58.5 4.6 %shard_map.74.refs_6_ = f32[4,512,128]{2,1,0:T(8,128)S(1)} custom-call(f32[4]{0:T(128)S(1)} %copy-done, s32[2]{0:T(128)S(1)} %pad_add_fusion.refs_1_, bf16[16,4,64,128]{3,2,1,0:T(8,128)(2,1)S(1)} %copy-done.3, bf16[16,4,64,128]{3,2,1,0:T(8,128)(2,1)S(1)} %copy-done.2, bf16[16,4,64,128]{3,2,1,0:T(8,128)(2,1)} %collective-permute-done.7.refs_4_, ...), custom_call_target="tpu_custom_call" | custom-call | flops 858993459200 | bytes 2516582400 | tf_op jit(solution)/shard_map/pallas_call | solution.py:309
  63.2 16.7 %all-to-all-done.received_ref.slots_ref = bf16[64,4,64,128]{3,2,1,0:T(8,128)(2,1)} async-done(((bf16[64,4,64,128]{3,2,1,0:T(8,128)(2,1)}), bf16[64,4,64,128]{3,2,1,0:T(8,128)(2,1)}, u32[]{:S(2)}, u32[]{:S(2)}) %all-to-all-start) | async-done | bytes 4194336 | tf_op jit(solution)/shard_map/all_to_all | solution.py:358
  79.9 3.0 %shard_map.72 = (bf16[16,2,64,128]{3,2,1,0:T(8,128)(2,1)}, bf16[16,2,64,128]{3,2,1,0:T(8,128)(2,1)}, bf16[16,2,64,128]{3,2,1,0:T(8,128)(2,1)}, bf16[16,2,64,128]{3,2,1,0:T(8,128)(2,1)}) custom-call(s32[64]{0:T(128)} %copy-done.8, s32[64]{0:T(128)} %broadcast_select_fusion.1.pick_ref, bf16[64,4,64,128]{3,2,1,0:T(8,128)(2,1)} %all-to-all-done.received_ref.slots_ref, ...), custom_call_target="tpu_custom_call" | custom-call | bytes 4194304 | tf_op jit(solution)/shard_map/pallas_call | solution.py:226
  83.0 3.1 %collective-permute-start.2 = (bf16[16,2,64,128]{3,2,1,0:T(8,128)(2,1)}, bf16[16,2,64,128]{3,2,1,0:T(8,128)(2,1)}, u32[]{:S(2)}, u32[]{:S(2)}) collective-permute-start(bf16[16,2,64,128]{3,2,1,0:T(8,128)(2,1)} %get-tuple-element.26), channel_id=1, source_target_pairs={{0,96},{32,0},{64,32},{96,64},{1,97},{33,1},{65,33},{97,65},{2,98}... | collective-permute-start | bytes 1572872 | tf_op jit(solution)/shard_map/ppermute | solution.py:322
  86.1 1.3 collective-permute-done.5.refs_4_
  88.2 3.4 %shard_map.75.refs_6_ = f32[4,512,128]{2,1,0:T(8,128)S(1)} custom-call(f32[4]{0:T(128)S(1)} %copy-done, s32[2]{0:T(128)S(1)} %pad_add_fusion.refs_1_, bf16[22,2,64,128]{3,2,1,0:T(8,128)(2,1)S(1)} %copy-done.4, bf16[22,2,64,128]{3,2,1,0:T(8,128)(2,1)} %collective-permute-done.4.refs_3_, bf16[22,2,64,128]{3,2,1,0:T(8,128)(2,1)} %collective-permute-done.5.refs_4_, ...), custom_call_target="tpu_custom_call" | custom-call | flops 590558003200 | bytes 1677721600 | tf_op jit(solution)/shard_map/pallas_call | solution.py:309
  91.6 7.4 %collective-permute-done.1.refs_3_ = bf16[16,2,64,128]{3,2,1,0:T(8,128)(2,1)} collective-permute-done((bf16[16,2,64,128]{3,2,1,0:T(8,128)(2,1)}, bf16[16,2,64,128]{3,2,1,0:T(8,128)(2,1)}, u32[]{:S(2)}, u32[]{:S(2)}) %collective-permute-start.1) | collective-permute-done | bytes 524320 | tf_op jit(solution)/shard_map/ppermute | solution.py:322
  99.0 11.0 %collective-permute-done.2.refs_4_ = bf16[16,2,64,128]{3,2,1,0:T(8,128)(2,1)} collective-permute-done((bf16[16,2,64,128]{3,2,1,0:T(8,128)(2,1)}, bf16[16,2,64,128]{3,2,1,0:T(8,128)(2,1)}, u32[]{:S(2)}, u32[]{:S(2)}) %collective-permute-start.2) | collective-permute-done | bytes 524320 | tf_op jit(solution)/shard_map/ppermute | solution.py:322
  110.0 1.1 collective-permute-done.3.refs_5_
  111.1 3.2 %shard_map.76 = (f32[1024,128]{1,0:T(8,128)S(1)}, f32[1024,128]{1,0:T(8,128)S(1)}) custom-call(f32[4]{0:T(128)S(1)} %copy-done, s32[2]{0:T(128)S(1)} %pad_add_fusion.refs_1_, bf16[16,2,64,128]{3,2,1,0:T(8,128)(2,1)S(1)} %copy-done.5, bf16[16,2,64,128]{3,2,1,0:T(8,128)(2,1)} %collective-permute-done.1.refs_3_, ...), custom_call_target="tpu_custom_call" | custom-call | flops 1073741824 | bytes 4194304 | tf_op jit(solution)/shard_map/pallas_call | solution.py:309
  115.2 1.5 %collective-permute-done.9 = f32[1024,128]{1,0:T(8,128)S(1)} collective-permute-done((f32[1024,128]{1,0:T(8,128)S(1)}, f32[1024,128]{1,0:T(8,128)S(1)}, u32[]{:S(2)}, u32[]{:S(2)}) %collective-permute-start.9) | collective-permute-done | bytes 524320 | tf_op jit(solution)/shard_map/ppermute | solution.py:370
  117.6 8.8 %all-to-all-start.1 = ((f32[64,16,128]{2,1,0:T(8,128)}), f32[64,16,128]{2,1,0:T(8,128)S(1)}, u32[]{:S(2)}, u32[]{:S(2)}) async-start(f32[64,16,128]{2,1,0:T(8,128)} %bitcast.4), calls=%async_computation.1 | async-start | bytes 1048576 | tf_op jit(solution)/shard_map/all_to_all | solution.py:371
  126.4 3.3 %shard_map.77 = bf16[4,64,64,128]{3,2,1,0:T(8,128)(2,1)} custom-call(bf16[64,4,64,128]{3,2,1,0:T(8,128)(2,1)} %all-to-all-done.received_ref.slots_ref), custom_call_target="tpu_custom_call" | custom-call | bytes 8388608 | tf_op jit(solution)/shard_map/pallas_call | solution.py:250
  129.7 8.9 %all-to-all-done.1 = f32[64,16,128]{2,1,0:T(8,128)S(1)} async-done(((f32[64,16,128]{2,1,0:T(8,128)}), f32[64,16,128]{2,1,0:T(8,128)S(1)}, u32[]{:S(2)}, u32[]{:S(2)}) %all-to-all-start.1) | async-done | bytes 524320 | tf_op jit(solution)/shard_map/all_to_all | solution.py:371
  (55 shorter events, 11.9 us)
Async XLA Ops:
  0.7 44.2 %copy-start.8 = (s32[64]{0:T(128)}, s32[64]{0:T(128)S(1)}, u32[]{:S(2)}) copy-start(s32[64]{0:T(128)S(1)} %get-tuple-element.38.order_ref) | copy-start | bytes 772
  2.4 7.5 %copy-start.6 = (s32[768]{0:T(1024)S(1)}, s32[768]{0:T(1024)}, u32[]{:S(2)}) copy-start(s32[768]{0:T(1024)} %param.7) | copy-start | bytes 9220
  5.3 40.2 %collective-permute-start = (bf16[16,4,64,128]{3,2,1,0:T(8,128)(2,1)}, bf16[16,4,64,128]{3,2,1,0:T(8,128)(2,1)S(1)}, u32[]{:S(2)}, u32[]{:S(2)}) collective-permute-start(bf16[16,4,64,128]{3,2,1,0:T(8,128)(2,1)} %shard_map.68.refs_4_), channel_id=1, source_target_pairs={{0,64},{32,96},{64,0},{96,32},{1,65},{33,97},{65,1},{97,33},{2,66}... | collective-permute-start | bytes 3145736 | tf_op jit(solution)/shard_map/ppermute | solution.py:322
  10.2 0.7 copy-start.7
  19.5 60.3 %all-to-all-start = ((bf16[64,4,64,128]{3,2,1,0:T(8,128)(2,1)}), bf16[64,4,64,128]{3,2,1,0:T(8,128)(2,1)}, u32[]{:S(2)}, u32[]{:S(2)}) async-start(bf16[64,4,64,128]{3,2,1,0:T(8,128)(2,1)} %get-tuple-element.21), calls=%async_computation | async-start | bytes 8388608 | tf_op jit(solution)/shard_map/all_to_all | solution.py:358
  30.9 25.6 %collective-permute-start.7 = (bf16[16,4,64,128]{3,2,1,0:T(8,128)(2,1)}, bf16[16,4,64,128]{3,2,1,0:T(8,128)(2,1)}, u32[]{:S(2)}, u32[]{:S(2)}) collective-permute-start(bf16[16,4,64,128]{3,2,1,0:T(8,128)(2,1)} %get-tuple-element.32), channel_id=1, source_target_pairs={{0,96},{32,0},{64,32},{96,64},{1,97},{33,1},{65,33},{97,65},{2,98}... | collective-permute-start | bytes 3145736 | tf_op jit(solution)/shard_map/ppermute | solution.py:322
  31.4 25.9 %collective-permute-start.8 = (bf16[16,4,64,128]{3,2,1,0:T(8,128)(2,1)}, bf16[16,4,64,128]{3,2,1,0:T(8,128)(2,1)}, u32[]{:S(2)}, u32[]{:S(2)}) collective-permute-start(bf16[16,4,64,128]{3,2,1,0:T(8,128)(2,1)} %get-tuple-element.33), channel_id=1, source_target_pairs={{0,32},{32,64},{64,96},{96,0},{1,33},{33,65},{65,97},{97,1},{2,34}... | collective-permute-start | bytes 3145736 | tf_op jit(solution)/shard_map/ppermute | solution.py:322
  41.7 44.4 %collective-permute-start.4 = (bf16[22,2,64,128]{3,2,1,0:T(8,128)(2,1)}, bf16[22,2,64,128]{3,2,1,0:T(8,128)(2,1)}, u32[]{:S(2)}, u32[]{:S(2)}) collective-permute-start(bf16[22,2,64,128]{3,2,1,0:T(8,128)(2,1)} %get-tuple-element.28), channel_id=1, source_target_pairs={{0,64},{32,96},{64,0},{96,32},{1,65},{33,97},{65,1},{97,33},{2,66}... | collective-permute-start | bytes 2162696 | tf_op jit(solution)/shard_map/ppermute | solution.py:322
  42.8 44.6 %collective-permute-start.5 = (bf16[22,2,64,128]{3,2,1,0:T(8,128)(2,1)}, bf16[22,2,64,128]{3,2,1,0:T(8,128)(2,1)}, u32[]{:S(2)}, u32[]{:S(2)}) collective-permute-start(bf16[22,2,64,128]{3,2,1,0:T(8,128)(2,1)} %get-tuple-element.29), channel_id=1, source_target_pairs={{0,96},{32,0},{64,32},{96,64},{1,97},{33,1},{65,33},{97,65},{2,98}... | collective-permute-start | bytes 2162696 | tf_op jit(solution)/shard_map/ppermute | solution.py:322
  45.6 1.0 copy-start.1
  45.6 42.6 %collective-permute-start.6 = (bf16[22,2,64,128]{3,2,1,0:T(8,128)(2,1)}, bf16[22,2,64,128]{3,2,1,0:T(8,128)(2,1)}, u32[]{:S(2)}, u32[]{:S(2)}) collective-permute-start(bf16[22,2,64,128]{3,2,1,0:T(8,128)(2,1)} %get-tuple-element.30), channel_id=1, source_target_pairs={{0,32},{32,64},{64,96},{96,0},{1,33},{33,65},{65,97},{97,1},{2,34}... | collective-permute-start | bytes 2162696 | tf_op jit(solution)/shard_map/ppermute | solution.py:322
  46.6 10.8 %copy-start = (f32[4]{0:T(128)S(1)}, f32[4]{0:T(128)}, u32[]{:S(2)}) copy-start(f32[4]{0:T(128)} %refs_0_.5) | copy-start | bytes 52
  46.6 10.8 %copy-start.3 = (bf16[16,4,64,128]{3,2,1,0:T(8,128)(2,1)S(1)}, bf16[16,4,64,128]{3,2,1,0:T(8,128)(2,1)}, u32[]{:S(2)}) copy-start(bf16[16,4,64,128]{3,2,1,0:T(8,128)(2,1)} %get-tuple-element.31.refs_2_) | copy-start | bytes 3145732
  57.3 1.2 copy-start.2
  63.2 25.0 %copy-start.4 = (bf16[22,2,64,128]{3,2,1,0:T(8,128)(2,1)S(1)}, bf16[22,2,64,128]{3,2,1,0:T(8,128)(2,1)}, u32[]{:S(2)}) copy-start(bf16[22,2,64,128]{3,2,1,0:T(8,128)(2,1)} %get-tuple-element.23.refs_1_.refs_2_) | copy-start | bytes 2162692
  82.9 16.1 %collective-permute-start.1 = (bf16[16,2,64,128]{3,2,1,0:T(8,128)(2,1)}, bf16[16,2,64,128]{3,2,1,0:T(8,128)(2,1)}, u32[]{:S(2)}, u32[]{:S(2)}) collective-permute-start(bf16[16,2,64,128]{3,2,1,0:T(8,128)(2,1)} %get-tuple-element.25), channel_id=1, source_target_pairs={{0,64},{32,96},{64,0},{96,32},{1,65},{33,97},{65,1},{97,33},{2,66}... | collective-permute-start | bytes 1572872 | tf_op jit(solution)/shard_map/ppermute | solution.py:322
  83.0 27.0 %collective-permute-start.2 = (bf16[16,2,64,128]{3,2,1,0:T(8,128)(2,1)}, bf16[16,2,64,128]{3,2,1,0:T(8,128)(2,1)}, u32[]{:S(2)}, u32[]{:S(2)}) collective-permute-start(bf16[16,2,64,128]{3,2,1,0:T(8,128)(2,1)} %get-tuple-element.26), channel_id=1, source_target_pairs={{0,96},{32,0},{64,32},{96,64},{1,97},{33,1},{65,33},{97,65},{2,98}... | collective-permute-start | bytes 1572872 | tf_op jit(solution)/shard_map/ppermute | solution.py:322
  86.1 25.0 %collective-permute-start.3 = (bf16[16,2,64,128]{3,2,1,0:T(8,128)(2,1)}, bf16[16,2,64,128]{3,2,1,0:T(8,128)(2,1)}, u32[]{:S(2)}, u32[]{:S(2)}) collective-permute-start(bf16[16,2,64,128]{3,2,1,0:T(8,128)(2,1)} %get-tuple-element.27), channel_id=1, source_target_pairs={{0,32},{32,64},{64,96},{96,0},{1,33},{33,65},{65,97},{97,1},{2,34}... | collective-permute-start | bytes 1572872 | tf_op jit(solution)/shard_map/ppermute | solution.py:322
  88.2 22.9 %copy-start.5 = (bf16[16,2,64,128]{3,2,1,0:T(8,128)(2,1)S(1)}, bf16[16,2,64,128]{3,2,1,0:T(8,128)(2,1)}, u32[]{:S(2)}) copy-start(bf16[16,2,64,128]{3,2,1,0:T(8,128)(2,1)} %get-tuple-element.24.refs_2_) | copy-start | bytes 1572868
  114.4 2.4 %collective-permute-start.9 = (f32[1024,128]{1,0:T(8,128)S(1)}, f32[1024,128]{1,0:T(8,128)S(1)}, u32[]{:S(2)}, u32[]{:S(2)}) collective-permute-start(f32[1024,128]{1,0:T(8,128)S(1)} %get-tuple-element.35), channel_id=1, source_target_pairs={{0,1},{1,0},{2,3},{3,2},{4,5},{5,4},{6,7},{7,6},{8,9},{9,8},{10,11... | collective-permute-start | bytes 1572872 | tf_op jit(solution)/shard_map/ppermute | solution.py:370
  117.6 21.0 %all-to-all-start.1 = ((f32[64,16,128]{2,1,0:T(8,128)}), f32[64,16,128]{2,1,0:T(8,128)S(1)}, u32[]{:S(2)}, u32[]{:S(2)}) async-start(f32[64,16,128]{2,1,0:T(8,128)} %bitcast.4), calls=%async_computation.1 | async-start | bytes 1048576 | tf_op jit(solution)/shard_map/all_to_all | solution.py:371
